TPU v7x, 32 devices: a whole 2x2x4 slice. The times are simulated.
32 devices in a mesh: section: 2 (over x), dp: 16 (over z, y, core).
Axes of the slice: x: 2, y: 2, z: 4, core: 2. Of those that a mesh axis runs over, the one named last changes fastest.
Arguments:
- embeds: bfloat16 [2, 32, 1024, 512], P('section', 'dp'), may hold values from -6 to 6
- cotangent: bfloat16 [2, 32, 1024, 512], P('section', 'dp'), may hold values from -6 to 6
- pair_ids: int32 [32], P('dp'), may hold values from 0 to 15
- seq_lengths: int32 [2, 32], P(None, 'dp'), may hold values from 512 to 1024, as said below
- alive_count: int32 [16], P('dp'), may hold values from 1 to 2, as said below
- self_proj: bfloat16 [2, 3, 512, 512], P('section'), may hold values from -0.25 to 0.25
- self_out: bfloat16 [2, 512, 512], P('section'), may hold values from -2 to 2
- self_bias: float32 [2, 3, 512], P('section'), may hold values from -1.75 to 1.75
- ffn_in: bfloat16 [2, 512, 2048], P('section'), may hold values from -0.25 to 0.25
- ffn_in_bias: float32 [2, 2048], P('section'), may hold values from -1.75 to 1.75
- ffn_out: bfloat16 [2, 2048, 512], P('section'), may hold values from -0.125 to 0.125
- ffn_out_bias: float32 [2, 512], P('section'), may hold values from -1.75 to 1.75
- norm_gain: float32 [2, 2, 512], P('section'), may hold values from 0.5 to 1.5
- norm_bias: float32 [2, 2, 512], P('section'), may hold values from -1.75 to 1.75
- cross_proj: bfloat16 [3, 512, 512], replicated, may hold values from -0.25 to 0.25
- cross_out: bfloat16 [512, 512], replicated, may hold values from -2 to 2
- cross_bias: float32 [3, 512], replicated, may hold values from -1.75 to 1.75
- cross_norm_gain: float32 [512], replicated, may hold values from 0.5 to 1.5
- cross_norm_bias: float32 [512], replicated, may hold values from -1.75 to 1.75
- pair_embed: float32 [16, 512], replicated, may hold values from -3 to 3
Outputs:
- layer_out: bfloat16 [2, 32, 1024, 512], P('section', 'dp')
- embeds_grad: float32 [2, 32, 1024, 512], P('section', 'dp')
- self_proj_grad: float32 [2, 3, 512, 512], P('section')
- self_out_grad: float32 [2, 512, 512], P('section')
- self_bias_grad: float32 [2, 3, 512], P('section')
- ffn_in_grad: float32 [2, 512, 2048], P('section')
- ffn_in_bias_grad: float32 [2, 2048], P('section')
- ffn_out_grad: float32 [2, 2048, 512], P('section')
- ffn_out_bias_grad: float32 [2, 512], P('section')
- norm_gain_grad: float32 [2, 2, 512], P('section')
- norm_bias_grad: float32 [2, 2, 512], P('section')
- cross_proj_grad: float32 [3, 512, 512], replicated
- cross_out_grad: float32 [512, 512], replicated
- cross_bias_grad: float32 [3, 512], replicated
- cross_norm_gain_grad: float32 [512], replicated
- cross_norm_bias_grad: float32 [512], replicated
- pair_embed_grad: float32 [16, 512], replicated
Inputs may be any that keep to these rules, and one draw needn't show every extreme that they name: `seq_lengths`: in each row some sequence has exactly 1024 tokens. `alive_count`: sequence slots of a device at or past its count are padding; some device is full.
All inputs are finite; a program needn't handle non-finite values.
Results may differ from a plain program's by a relative error of at most 0.014.
Values may be sent and summed in bfloat16 or wider, within the bound.
A program may use at most 320 MiB of HBM per device.

v0:
```python
import functools

import jax
import jax.numpy as jnp
import numpy as np
from jax import lax
from jax.experimental import pallas as pl
from jax.experimental.pallas import tpu as pltpu
from jax.sharding import PartitionSpec as P

BF = jnp.bfloat16
F32 = jnp.float32
HEADS = 8
PAIRS = 16
MESH = pl.DeviceIdType.MESH
EPSILON = 1e-05
BLOCKED = -1e30
RB = 512
NN = (((1,), (0,)), ((), ()))
NT = (((1,), (1,)), ((), ()))
TN = (((0,), (0,)), ((), ()))


def dot(left, right, dims=NN):
    return lax.dot_general(left, right, dims, preferred_element_type=F32)


def row_block(index, size=RB):
    return pl.ds(pl.multiple_of(index * size, size), size)


def loop(count, body, unroll=1):
    def step(index, carry):
        body(index)
        return carry

    lax.fori_loop(0, count, step, 0, unroll=unroll)


def lanes_of(half):
    lane = lax.broadcasted_iota(jnp.int32, (1, 128), 1)
    inside = (lane // 64) == half
    spare = lane - 64 * (1 - half)
    ones = (~inside) & (spare < 32)
    block = (~inside) & (spare >= 32)
    flag = (~inside) & (spare == 32)
    return tuple(m.astype(F32) for m in (inside, ones, block, flag))


def norm_rows(value):
    centre = jnp.mean(value, -1, keepdims=True)
    centred = value - centre
    rstd = lax.rsqrt(jnp.mean(centred * centred, -1, keepdims=True) + EPSILON)
    return centred * rstd, rstd


def norm_rows_back(normed, rstd, gain, grad):
    scaled = grad * gain
    return rstd * (
        scaled
        - jnp.mean(scaled, -1, keepdims=True)
        - normed * jnp.mean(scaled * normed, -1, keepdims=True)
    )


def gelu_both(hidden):
    phi = 0.5 + 0.5 * lax.erf(hidden * 0.7071067811865476)
    bell = jnp.exp(-0.5 * hidden * hidden)
    return hidden * phi, phi + hidden * (bell * 0.3989422804014327)


def key_fill(count, length, ones, block):
    position = lax.broadcasted_iota(jnp.int32, (count, 128), 0)
    return ones + jnp.where(position < length, 0.0, BLOCKED) * block


def causal_cut(scores, query_axis):
    query = lax.broadcasted_iota(jnp.int32, scores.shape, query_axis)
    key = lax.broadcasted_iota(jnp.int32, scores.shape, 1 - query_axis)
    return jnp.where(key <= query, scores, BLOCKED)


def mix_forward(queries, keys, values_t, length, causal, mixed_t, lse):
    count = queries.shape[0]
    span = keys.shape[0]
    size = min(512 if causal else 1024, count)

    def pair(index):
        cols = row_block(index, 128)
        q = queries[:, cols].astype(F32) * 0.125
        k = keys[:, cols].astype(F32)
        vt = values_t[cols, :].astype(F32)
        lane = lax.broadcasted_iota(jnp.int32, (128, 1), 0)
        qa, ka, va = [], [], []
        for half in range(2):
            inside, ones, block, flag = lanes_of(half)
            qa.append((q * inside + flag).astype(BF))
            ka.append((k * inside + key_fill(span, length, ones, block)).astype(BF))
            va.append(jnp.where((lane // 64) == half, vt, 1.0).astype(BF))

        def scores_of(part, half):
            here = slice(part * size, (part + 1) * size)
            pieces = [(0, part * size, False), (part * size, size, True)] if causal else [(0, span, False)]
            return [
                (start, reach, cut, dot(ka[half][start : start + reach], qa[half][here], NT))
                for start, reach, cut in pieces
                if reach
            ]

        def finish(part, half, scores):
            here = slice(part * size, (part + 1) * size)
            scores = [(start, reach, causal_cut(s, 1) if cut else s) for start, reach, cut, s in scores]
            top = None
            for _, _, s in scores:
                best = jnp.max(s, axis=0, keepdims=True)
                top = best if top is None else jnp.maximum(top, best)
            total = None
            for start, reach, s in scores:
                o = dot(va[half][:, start : start + reach], jnp.exp(s - top).astype(BF))
                total = o if total is None else total + o
            other = 64 * (1 - half)
            mass = total[other : other + 1]
            own = total[64 * half : 64 * half + 64] / mass
            mixed_t[pl.ds(pl.multiple_of(index * 128 + 64 * half, 64), 64), here] = own.astype(BF)
            lse[index * 2 + half, :, here] = top + jnp.log(mass)

        waiting = None
        for tile in [(part, half) for part in range(count // size) for half in range(2)]:
            scores = scores_of(*tile)
            if waiting:
                finish(*waiting)
            waiting = (*tile, scores)
        finish(*waiting)

    loop(4, pair, 2)


def split3(value):
    high = value.astype(BF).astype(F32)
    middle = (value - high).astype(BF).astype(F32)
    low = (value - high - middle).astype(BF).astype(F32)
    return high, middle, low


def place_matrix():
    out = np.zeros((16, 512), np.float32)
    for half in range(2):
        other = 64 * (1 - half)
        for piece in range(3):
            out[half * 4 + piece, half * 128 + other + piece] = 1
            out[8 + half * 4 + piece, 256 + half * 128 + other + piece] = 1
        out[half * 4 + 3, half * 128 + other + 32] = 1
    return out


def mix_back(queries, keys, values, mixed_t, lse, grad_mixed, place, length, causal, d_q, d_k, d_v):
    count = queries.shape[0]
    span = keys.shape[0]
    size = 256 if causal else min(512, count)

    def pair(index):
        cols = row_block(index, 128)
        q = queries[:, cols].astype(F32) * 0.125
        k_low = keys[:, cols]
        k = k_low.astype(F32)
        v = values[:, cols].astype(F32)
        g_low = grad_mixed[:, cols]
        g = g_low.astype(F32)
        q_t = q.astype(BF).T
        g_t = g_low.T
        product = g_t.astype(F32) * mixed_t[cols, :].astype(F32)
        row = lax.broadcasted_iota(jnp.int32, (16, count), 0)
        spread = jnp.where((row == 3) | (row == 7), 1.0, 0.0)
        for half in range(2):
            shift = -lse[index * 2 + half]
            delta = -jnp.sum(product[64 * half : 64 * half + 64], axis=0, keepdims=True)
            for base, value in ((0, shift), (8, delta)):
                for piece, part in enumerate(split3(value)):
                    spread = jnp.where(row == base + 4 * half + piece, part, spread)
        extra = dot(spread.astype(BF), place[...], TN)
        qa, ka, va, ga = [], [], [], []
        for half in range(2):
            inside, ones, block, flag = lanes_of(half)
            qa.append((q * inside + extra[:, half * 128 : half * 128 + 128]).astype(BF))
            ga.append((g * inside + extra[:, 256 + half * 128 : 384 + half * 128]).astype(BF))
            ka.append((k * inside + key_fill(span, length, ones, block)).astype(BF))
            va.append((v * inside + (1.0 - inside)).astype(BF))
        lane = lax.broadcasted_iota(jnp.int32, (size, 128), 1)
        total_k = [None, None]
        total_v = [None, None]

        def grow(total, value):
            if total is None:
                return value
            if total.shape == value.shape:
                return total + value
            known = total.shape[1]
            return jnp.concatenate([total + value[:, :known], value[:, known:]], axis=1)

        for part in range(count // size):
            here = slice(part * size, (part + 1) * size)
            reach = (part + 1) * size if causal else span
            out_q = []
            for half in range(2):
                s = dot(qa[half][here], ka[half][:reach], NT)
                if causal:
                    if part:
                        s = jnp.concatenate([s[:, : part * size], causal_cut(s[:, part * size :], 0)], axis=1)
                    else:
                        s = causal_cut(s, 0)
                probs = jnp.exp(s)
                grads = dot(ga[half][here], va[half][:reach], NT)
                probs_low = probs.astype(BF)
                d_s = (probs * grads).astype(BF)
                total_v[half] = grow(total_v[half], dot(g_t[:, here], probs_low))
                total_k[half] = grow(total_k[half], dot(q_t[:, here], d_s))
                out_q.append(dot(d_s, k_low[:reach]))
            d_q[here, cols] = (jnp.where(lane < 64, out_q[0], out_q[1]) * 0.125).astype(BF)
        for target, total in ((d_k, total_k), (d_v, total_v)):
            joined = jnp.concatenate([total[0][:64], total[1][64:]], axis=0).astype(BF)
            target[:, cols] = joined.T

    loop(4, pair, 2)


class Late:
    def __init__(self, ref, copy):
        self.ref, self.copy = ref, copy

    def get(self):
        if self.copy is not None:
            self.copy.wait()
            self.copy = None
        return self.ref


class Limits:
    def __init__(self, ref, picks):
        self.ref, self.picks = ref, picks

    def __getitem__(self, index):
        if len(self.picks) == 2:
            near, far = self.picks
            return self.ref[near[index] + lax.axis_index("section") * (far[index] - near[index])]
        return self.ref[self.picks[index]]


class Pieces:
    def __init__(self, source, ref, sem):
        self.source, self.ref, self.sem = source, ref, sem

    def wait(self):
        pltpu.make_async_copy(self.source.at[pl.ds(0, self.ref.shape[0])], self.ref, self.sem).wait()


class Leaving:
    def __init__(self, ref, out, sem):
        self.ref, self.out, self.sem = ref, out, sem

    def send(self, rows=None):
        if rows is None:
            pltpu.make_async_copy(self.ref, self.out, self.sem).start()
        else:
            pltpu.make_async_copy(self.ref.at[rows], self.out.at[rows], self.sem).start()

    def part(self, index):
        return Leaving(self.ref.at[index], self.out.at[index], self.sem)

    def finish(self):
        pltpu.make_async_copy(self.ref, self.out, self.sem).wait()


def sds(shape, dtype):
    return jax.ShapeDtypeStruct(shape, dtype)


def vm(shape, dtype):
    return pltpu.VMEM(shape, dtype)


def call(kernel, name, scalars, picks, args, outs, scratch, flops):
    anywhere = pl.BlockSpec(memory_space=pl.ANY)
    inside = pl.BlockSpec(memory_space=pltpu.VMEM)
    operands, in_specs, out_shapes, out_specs, memory, aliases = [], [], [], [], [], {}
    plan_in, plan_out, places = [], [], []
    for value, kind in args:
        places.append(len(operands))
        operands.append(value)
        if kind == "vmem":
            in_specs.append(inside)
            plan_in.append(None)
        else:
            in_specs.append(anywhere)
            if kind[0] == "either":
                _, index, other, other_index = kind
                plan_in.append((len(memory), (index, len(operands), other_index)))
                operands.append(other)
                in_specs.append(anywhere)
                memory.append(vm(value.shape if index is None else value.shape[1:], value.dtype))
                continue
            if kind[0] == "rows":
                plan_in.append((len(memory), kind[2]))
                memory.append(vm(kind[1], value.dtype))
                continue
            index = kind[1] if isinstance(kind, tuple) else None
            plan_in.append((len(memory), index))
            memory.append(vm(value.shape if index is None else value.shape[1:], value.dtype))
    for position, (shape, dtype, kind) in enumerate(outs):
        if kind == "vmem":
            out_shapes.append(sds(shape, dtype))
            out_specs.append(inside)
            plan_out.append(None)
            continue
        out_specs.append(anywhere)
        index, earlier = None, None
        if isinstance(kind, tuple) and kind[0] == "late":
            index, earlier, total = kind[1:]
            out_shapes.append(sds((total, *shape), dtype))
            if earlier is not None:
                aliases[len(operands)] = position
                operands.append(earlier)
                in_specs.append(anywhere)
        else:
            out_shapes.append(sds(shape, dtype))
        plan_out.append((len(memory), index, len(operands) if isinstance(kind, tuple) and kind[0] == "from" else None))
        memory.append(vm(shape, dtype))
        if isinstance(kind, tuple) and kind[0] == "from":
            operands.append(kind[1])
            in_specs.append(anywhere)
    total_in, count_out, count_memory = len(operands), len(outs), len(memory)

    def body(numbers, *refs):
        ins, results = refs[:total_in], refs[total_in : total_in + count_out]
        held = refs[total_in + count_out : total_in + count_out + count_memory]
        own = refs[total_in + count_out + count_memory : -1]
        sems = refs[-1]
        first, last = [], []
        for spot, plan in zip(places, plan_in):
            ref = ins[spot]
            if plan is None:
                first.append(ref)
                continue
            where, index = plan
            if isinstance(index, tuple):
                index, other, other_index = index
                copies = [
                    pltpu.make_async_copy(r if i is None else r.at[i], held[where], sems.at[where])
                    for r, i in ((ref, index), (ins[other], other_index))
                ]
                section = lax.axis_index("section")
                pl.when(section == 0)(copies[0].start)
                pl.when(section == 1)(copies[1].start)
                first.append(Late(held[where], copies[0]))
                continue
            if isinstance(index, list):
                for begin, end, size in index:
                    pltpu.make_async_copy(ref.at[pl.ds(begin, size)], held[where].at[pl.ds(end, size)], sems.at[where]).start()
                first.append(Late(held[where], Pieces(ref, held[where], sems.at[where])))
                continue
            copy = pltpu.make_async_copy(ref if index is None else ref.at[index], held[where], sems.at[where])
            copy.start()
            first.append(Late(held[where], copy))
        for ref, plan in zip(results, plan_out):
            if plan is None:
                last.append(ref)
                continue
            where, index, source = plan
            leaving = Leaving(held[where], ref if index is None else ref.at[index], sems.at[where])
            if source is not None:
                copy = pltpu.make_async_copy(ins[source], held[where], sems.at[where])
                copy.start()
                leaving.begin = Late(held[where], copy)
            last.append(leaving)
        kernel(Limits(numbers, picks), *first, *last, *own)
        for leaving in last:
            if isinstance(leaving, Leaving):
                leaving.finish()

    return pl.pallas_call(
        body,
        name=name,
        out_shape=out_shapes,
        in_specs=[pl.BlockSpec(memory_space=pltpu.SMEM), *in_specs],
        out_specs=out_specs,
        scratch_shapes=[*memory, *[vm(*s) for s in scratch], pltpu.SemaphoreType.DMA((max(count_memory, 1),))],
        input_output_aliases={i + 1: o for i, o in aliases.items()},
        compiler_params=pltpu.CompilerParams(vmem_limit_bytes=62 * 2**20),
        cost_estimate=pl.CostEstimate(flops=int(flops), bytes_accessed=20 * 2**20, transcendentals=0),
    )(scalars, *operands)


def valid_rows(index, limit, size=RB):
    return (lax.broadcasted_iota(jnp.int32, (size, 1), 0) + index * size < limit).astype(F32)


def ffn_rows(z_low, w_in, c_in, w_out, c_out, act_ref, slope_ref, r, flipped=False):
    def hidden(c):
        cols = slice(c * 512, c * 512 + 512)
        return dot(z_low, w_in[cols], NT) + c_in[c : c + 1] if flipped else dot(z_low, w_in[:, cols]) + c_in[:, cols]

    total, coming = None, hidden(0)
    for c in range(4):
        cols = slice(c * 512, c * 512 + 512)
        here = coming
        coming = hidden(c + 1) if c < 3 else None
        act, slope = gelu_both(here)
        act = act.astype(BF)
        act_ref[r, cols] = act
        slope_ref[r, cols] = slope.astype(BF)
        part = dot(act, w_out[cols])
        total = part if total is None else total + part
    return total + c_out[...]


def put(target, rows, value, later):
    target[rows] = (value + target[rows].astype(F32) if later else value).astype(BF)


def ffn_back(grad_low, act, slope, z_low, w_in, w_out, put_rows, small, on_rows, flipped=False):
    def body(index):
        r = row_block(index)
        g = grad_low[r]
        total, coming = None, dot(g, w_out[0:512], NT)
        for c in range(4):
            cols = slice(c * 512, c * 512 + 512)
            here = coming
            coming = dot(g, w_out[512 * c + 512 : 512 * c + 1024], NT) if c < 3 else None
            dh = (here * slope[r, cols].astype(F32)).astype(BF)
            slope[r, cols] = dh
            small[3 + c : 4 + c] += jnp.sum(dh.astype(F32), axis=0, keepdims=True)
            part = dot(dh, w_in[cols]) if flipped else dot(dh, w_in[:, cols], NT)
            total = part if total is None else total + part
        small[7:8] += jnp.sum(g.astype(F32), axis=0, keepdims=True)
        on_rows(r, total)

    loop(grad_low.shape[0] // RB, body)
    z = z_low[...]
    g = grad_low[...]
    act = act.get() if isinstance(act, Late) else act
    for c in range(4):
        cols = slice(c * 512, c * 512 + 512)
        put_rows(c * 512, dot(z, slope[:, cols], TN))
        put_rows(2048 + c * 512, dot(act[:, cols], g, TN))


def project(count, x_low, proj, bias, q, k, v, v_t):
    def body(index):
        r = row_block(index)
        x = x_low(r)
        q.ref[r] = (dot(x, proj[0]) + bias[0:1]).astype(BF)
        k.ref[r] = dot(x, proj[1]).astype(BF)
        v.ref[r] = (dot(x, proj[2]) + bias[1:2]).astype(BF)

    loop(count // RB, body)
    q.send()
    k.send()
    v.send()
    v_t[...] = v.ref[...].T


def self_back(x, proj, out_w, q, k, v, mixed_t, lse, place, length, causal, grad_low, grad_mixed, d_q, d_k, d_v, pack, later, small, rest):
    grad_mixed[...] = dot(grad_low[...], out_w.get()[...], NT).astype(BF)
    mixed_t = mixed_t.get()
    if later:
        pack.begin.get()
    put(pack.ref, slice(1536, 2048), dot(mixed_t[...], grad_low[...]), later)
    q, k, v, x = q.get(), k.get(), v.get(), x.get()
    mix_back(q, k, v, mixed_t, lse, grad_mixed, place, length, causal, d_q, d_k, d_v)
    small[0:1] += jnp.sum(d_q[...].astype(F32), axis=0, keepdims=True)
    small[1:2] += jnp.sum(d_v[...].astype(F32), axis=0, keepdims=True)
    small[2:3] += jnp.sum(grad_low[...].astype(F32), axis=0, keepdims=True)
    xl = x[...]
    put(pack.ref, slice(0, 512), dot(xl, d_q[...], TN), later)
    put(pack.ref, slice(512, 1024), dot(xl, d_k[...], TN), later)
    put(pack.ref, slice(1024, 1536), dot(xl, d_v[...], TN), later)
    pack.send()
    proj = proj.get()

    def body(index):
        r = row_block(index)
        rest(r, dot(d_q[r], proj[0], NT) + dot(d_k[r], proj[1], NT) + dot(d_v[r], proj[2], NT))

    loop(x.shape[0] // RB, body)


def begin_small(small, earlier):
    small[...] = jnp.zeros(small.shape, F32) if earlier is None else earlier[...]


def enc_forward_kernel(
    length, x, proj, out_w, w_in, w_out, bias, c_in, c_out, gain, offset,
    memory, shown, q, k, v, mixed_t, lse, normed1, rstd1, act, slope, normed2, rstd2, v_t,
):
    x = x.get()
    project(x.shape[0], lambda r: x[r], proj.get(), bias, q, k, v, v_t)
    mix_forward(q.ref, k.ref, v_t, length[0], False, mixed_t.ref, lse)
    mixed_t.send()
    out_w, w_in, w_out = out_w.get(), w_in.get(), w_out.get()

    def body(index):
        r = row_block(index)
        xf = x[r].astype(F32)
        n1, s1 = norm_rows(xf + dot(mixed_t.ref[:, r], out_w[...], TN) + bias[2:3])
        normed1.ref[r] = n1.astype(BF)
        rstd1[r] = s1
        y = n1 * gain[0:1] + offset[0:1]
        f = ffn_rows(y.astype(BF), w_in, c_in, w_out, c_out, act.ref, slope.ref, r)
        n2, s2 = norm_rows(y + f + xf)
        normed2.ref[r] = n2.astype(BF)
        rstd2[r] = s2
        result = n2 * gain[1:2] + offset[1:2]
        memory.ref[r] = result.astype(BF)
        shown.ref[r] = (result * valid_rows(index, length[1])).astype(BF)
        for leaving in (act, slope, memory, shown, normed1, normed2):
            leaving.send(r)

    loop(x.shape[0] // RB, body)


def enc_forward(scalars, picks, x, s, layer, shown):
    proj, out_w, bias, w_in, c_in, w_out, c_out, gain, offset = layer
    count, n, d = x.shape
    f = w_in.shape[1]
    nd = (n, d)
    args = [(x, ("late", s)), (proj, "late"), (out_w, "late"), (w_in, "late"), (w_out, "late")]
    args += [(v, "vmem") for v in (bias, c_in, c_out, gain, offset)]
    outs = [
        (nd, BF, "late"), (nd, BF, ("late", s, shown, count)), (nd, BF, "late"), (nd, BF, "late"), (nd, BF, "late"), ((d, n), BF, "late"),
        ((8, 1, n), F32, "vmem"), (nd, BF, "late"), ((n, 1), F32, "vmem"), ((n, f), BF, "late"), ((n, f), BF, "late"), (nd, BF, "late"), ((n, 1), F32, "vmem"),
    ]
    return call(enc_forward_kernel, "encoder_forward", scalars, picks, args, outs, [((d, n), BF)], 15e9)


def enc_back_kernel(
    later, length, cot, d_memory, normed2, normed1, w_out, slope, w_in, act, out_w, mixed_t, q, k, v, x, proj,
    lse, rstd1, rstd2, gain, offset, place, *refs,
):
    earlier = refs[0] if later else None
    d_x, pack_a, pack_b, small, last, grad_low, z_low, grad_mixed, d_q, d_k, d_v = refs[later:]
    begin_small(small, earlier)
    cot, d_memory, normed2, normed1 = cot.get(), d_memory.get(), normed2.get(), normed1.get()

    def top(index):
        r = row_block(index)
        n2 = normed2[r].astype(F32)
        g = cot[r].astype(F32) * valid_rows(index, length[1]) + d_memory[r].astype(F32)
        small[9:10] += jnp.sum(g * n2, axis=0, keepdims=True)
        small[11:12] += jnp.sum(g, axis=0, keepdims=True)
        g = norm_rows_back(n2, rstd2[r], gain[1:2], g)
        last[r] = g
        grad_low[r] = g.astype(BF)
        z_low[r] = (normed1[r].astype(F32) * gain[0:1] + offset[0:1]).astype(BF)

    loop(last.shape[0] // RB, top)

    def middle(r, grad):
        n1 = normed1[r].astype(F32)
        g = last[r] + grad
        small[8:9] += jnp.sum(g * n1, axis=0, keepdims=True)
        small[10:11] += jnp.sum(g, axis=0, keepdims=True)
        g = norm_rows_back(n1, rstd1[r], gain[0:1], g)
        last[r] = last[r] + g
        grad_mixed[r] = g.astype(BF)

    def put_rows(start, value):
        if later:
            pack_b.begin.get()
        put(pack_b.ref, slice(start, start + 512), value, later)

    ffn_back(grad_low, act, slope.get(), z_low, w_in.get(), w_out.get(), put_rows, small, middle)
    pack_b.send()
    grad_low[...] = grad_mixed[...]

    def rest(r, grad):
        d_x.ref[r] = last[r] + grad
        d_x.send(r)

    self_back(x, proj, out_w, q, k, v, mixed_t, lse, place, length[0], False, grad_low, grad_mixed, d_q, d_k, d_v, pack_a, later, small, rest)


def enc_back(scalars, picks, x, s, d_memory, cot, layer, place, saved, prev):
    proj, out_w, bias, w_in, c_in, w_out, c_out, gain, offset = layer
    q, k, v, mixed_t, lse, normed1, rstd1, act, slope, normed2, rstd2 = saved
    count, n, d = x.shape
    f = w_in.shape[1]
    nd = (n, d)
    args = [(cot, ("late", s))]
    args += [(a, "late") for a in (d_memory, normed2, normed1, w_out, slope, w_in, act, out_w, mixed_t, q, k, v)]
    args += [(x, ("late", s)), (proj, "late")]
    args += [(a, "vmem") for a in (lse, rstd1, rstd2, gain, offset, place)]
    carry = lambda i: ("from", prev[i]) if prev else "late"
    if prev:
        args.append((prev[3], "vmem"))
    outs = [(nd, F32, ("late", s, prev[0] if prev else None, count)), ((4 * d, d), BF, carry(1)), ((2 * f, d), BF, carry(2)), ((16 + PAIRS, d), F32, "vmem")]
    scratch = [(nd, F32)] + [(nd, BF)] * 6
    return call(functools.partial(enc_back_kernel, bool(prev)), "encoder_back", scalars, picks, args, outs, scratch, 35e9)


def dec_self_kernel(length, x, proj, out_w, pair_table, bias, gain, offset, x_low, q, k, v, mixed_t, lse, normed1, rstd1, v_t):
    x = x.get()
    pair_row = pair_table[pl.ds(length[2], 1)]

    def low(r):
        value = (x[r].astype(F32) + pair_row).astype(BF)
        x_low.ref[r] = value
        return value

    project(x.shape[0], low, proj.get(), bias, q, k, v, v_t)
    x_low.send()
    mix_forward(q.ref, k.ref, v_t, length[0], True, mixed_t.ref, lse)
    mixed_t.send()
    out_w = out_w.get()

    def body(index):
        r = row_block(index)
        n1, s1 = norm_rows(x[r].astype(F32) + pair_row + dot(mixed_t.ref[:, r], out_w[...], TN) + bias[2:3])
        normed1.ref[r] = n1.astype(normed1.ref.dtype)
        rstd1[r] = s1
        normed1.send(r)

    loop(x.shape[0] // RB, body)


def dec_self(scalars, picks, x, s, pair_table, layer):
    proj, out_w, bias, w_in, c_in, w_out, c_out, gain, offset = layer
    count, n, d = x.shape
    nd = (n, d)
    args = [(x, ("late", s)), (proj, "late"), (out_w, "late")]
    args += [(v, "vmem") for v in (pair_table, bias, gain, offset)]
    outs = [(nd, BF, "late")] * 4 + [((d, n), BF, "late"), ((8, 1, n), F32, "vmem"), (nd, BF, "late"), ((n, 1), F32, "vmem")]
    return call(dec_self_kernel, "decoder_self", scalars, picks, args, outs, [((d, n), BF)], 8e9)


def padded(rows, count):
    return -(-rows // (16 * count)) * (16 * count)


def cross_rows(count, d):
    return padded(4 * d + 16, count)


def dec_mid_kernel(
    share_b, share_c, length, normed1, c_proj, memory, c_out, w_in, w_out, x, cot,
    pair_table, c_bias, c_gain, c_offset, vectors, place,
    shown, two, d_memory, pack,
    small, last, top, y_low, z_low, q, k, v, v_t, mixed_t, lse, normed2, rstd2, act, slope, grad_low, grad_mixed, d_q, d_k, d_v,
):
    small[...] = jnp.zeros(small.shape, F32)
    grad_last, grad_first = (two.part(i) for i in range(2))
    c_in, c_out_b, gain, offset = vectors[0:4], vectors[4:5], vectors[5:7], vectors[7:9]
    pair_row = pair_table[pl.ds(length[2], 1)]

    def put_part(start, value, share, shift):
        value = value.astype(BF)
        done = 0
        while done < value.shape[0]:
            owner, inner = divmod(start + done, share)
            size = min(share - inner, value.shape[0] - done)
            begin = owner * (share_b + share_c) + shift + inner
            pack.ref[begin : begin + size] = value[done : done + size]
            done += size

    def put_b(start, value):
        put_part(start, value, share_b, 0)

    def put_c(start, value):
        put_part(start, value, share_c, share_b)

    normed1, c_proj = normed1.get(), c_proj.get()
    count = normed1.shape[0]

    def queries(index):
        r = row_block(index)
        y = (normed1[r].astype(F32) * gain[0:1] + offset[0:1]).astype(BF)
        y_low[r] = y
        q[r] = (dot(y, c_proj[0]) + c_bias[0:1]).astype(BF)

    loop(count // RB, queries)
    memory = memory.get()
    span = memory.shape[0]

    def keys(index):
        r = row_block(index)
        m = memory[r]
        k[r] = dot(m, c_proj[1]).astype(BF)
        v[r] = (dot(m, c_proj[2]) + c_bias[1:2]).astype(BF)

    loop(span // RB, keys)
    v_t[...] = v[...].T
    mix_forward(q, k, v_t, length[0], False, mixed_t, lse)
    c_out, w_in, w_out, x, cot = c_out.get(), w_in.get(), w_out.get(), x.get(), cot.get()

    def forward(index):
        r = row_block(index)
        y = normed1[r].astype(F32) * gain[0:1] + offset[0:1]
        n2, s2 = norm_rows(y + dot(mixed_t[:, r], c_out[...], TN) + c_bias[2:3])
        normed2[r] = n2.astype(BF)
        rstd2[r] = s2
        z = n2 * c_gain[...] + c_offset[...]
        zl = z.astype(BF)
        z_low[r] = zl
        f = ffn_rows(zl, w_in, c_in, w_out, c_out_b, act, slope, r, True)
        n3, s3 = norm_rows(z + f + x[r].astype(F32) + pair_row)
        valid = valid_rows(index, length[1])
        shown.ref[r] = ((n3 * gain[1:2] + offset[1:2]) * valid).astype(BF)
        shown.send(r)
        g = cot[r].astype(F32) * valid
        small[9:10] += jnp.sum(g * n3, axis=0, keepdims=True)
        small[11:12] += jnp.sum(g, axis=0, keepdims=True)
        g = norm_rows_back(n3, s3, gain[1:2], g)
        last[r] = g
        grad_last.ref[r] = g.astype(BF)

    loop(count // RB, forward)
    grad_last.send()

    def middle(r, grad):
        n2 = normed2[r].astype(F32)
        g = last[r] + grad
        small[8:9] += jnp.sum(g * n2, axis=0, keepdims=True)
        small[10:11] += jnp.sum(g, axis=0, keepdims=True)
        g = norm_rows_back(n2, rstd2[r], c_gain[...], g)
        top[r] = g
        grad_low[r] = g.astype(BF)

    ffn_back(grad_last.ref, act, slope, z_low, w_in, w_out, put_b, small, middle, True)
    grad_mixed[...] = dot(grad_low[...], c_out[...], NT).astype(BF)
    put_c(1536, dot(mixed_t[...], grad_low[...]))
    mix_back(q, k, v, mixed_t, lse, grad_mixed, place, length[0], False, d_q, d_k, d_v)

    def back(index):
        r = row_block(index)
        d_memory.ref[r] = (dot(d_k[r], c_proj[1], NT) + dot(d_v[r], c_proj[2], NT)).astype(BF)
        d_memory.send(r)

    loop(span // RB, back)

    def first(index):
        r = row_block(index)
        grad_first.ref[r] = (top[r] + dot(d_q[r], c_proj[0], NT)).astype(BF)
        grad_first.send(r)

    loop(count // RB, first)
    small[0:1] += jnp.sum(d_q[...].astype(F32), axis=0, keepdims=True)
    small[1:2] += jnp.sum(d_v[...].astype(F32), axis=0, keepdims=True)
    small[2:3] += jnp.sum(grad_low[...].astype(F32), axis=0, keepdims=True)
    m = memory[...]
    put_c(0, dot(y_low[...], d_q[...], TN))
    put_c(512, dot(m, d_k[...], TN))
    put_c(1024, dot(m, d_v[...], TN))
    total_c = pack.ref.shape[0] // (share_b + share_c) * share_c
    put_c(2048, jnp.concatenate([small[...], jnp.zeros((total_c - 2064, 512), F32)]))
    pack.send()


def dec_mid(scalars, picks, x, cot, normed1, memory, pair_table, weights, vectors, cross, place, count):
    c_proj, c_out_w, c_bias, c_gain, c_offset = cross
    n, d = normed1[0].shape
    m = memory[0].shape[0]
    f = weights.shape[0] // 2
    nd, md = (n, d), (m, d)
    part = f // count
    share_b, share_c = 2 * f // count, cross_rows(count, d) // count
    args = [(normed1[0], ("either", None, normed1[1], None)), (c_proj, "late")]
    args += [(memory[0], ("either", None, memory[1], None)), (c_out_w, "late")]
    args += [(weights, ("rows", (f, d), [(2 * part * i + part * j, part * i, part) for i in range(count)])) for j in range(2)]
    args += [(v[0][0], ("either", v[0][1], v[1][0], v[1][1])) for v in (x, cot)]
    args += [(a, "vmem") for a in (pair_table, c_bias, c_gain, c_offset, vectors, place)]
    outs = [(nd, BF, "late"), ((2, n, d), BF, "late"), (md, BF, "late"), ((count * (share_b + share_c), d), BF, "late")]
    scratch = [((16, d), F32), (nd, F32), (nd, F32), (nd, BF), (nd, BF), (nd, BF), (md, BF), (md, BF), ((d, m), BF), ((d, n), BF)]
    scratch += [((8, 1, n), F32), (nd, BF), ((n, 1), F32), ((n, f), BF), ((n, f), BF), (nd, BF), (nd, BF), (nd, BF), (md, BF), (md, BF)]
    return call(functools.partial(dec_mid_kernel, share_b, share_c), "decoder_middle", scalars, picks, args, outs, scratch, 55e9)


def dec_self_back_kernel(
    later, length, grad_first, normed1, grad_last, out_w, mixed_t, q, k, v, x_low, proj,
    lse, rstd1, gain, place, *refs,
):
    earlier = refs[0] if later else None
    d_x, pack_a, small, last, grad_low, grad_mixed, d_q, d_k, d_v, column = refs[later:]
    begin_small(small, earlier)
    column[...] = jnp.zeros(column.shape, F32)
    grad_first, normed1, grad_last = grad_first.get(), normed1.get(), grad_last.get()

    def top(index):
        r = row_block(index)
        n1 = normed1[r].astype(F32)
        g = grad_first[r].astype(F32)
        small[8:9] += jnp.sum(g * n1, axis=0, keepdims=True)
        small[10:11] += jnp.sum(g, axis=0, keepdims=True)
        g = norm_rows_back(n1, rstd1[r], gain[0:1], g)
        last[r] = grad_last[r].astype(F32) + g
        grad_low[r] = g.astype(BF)

    loop(last.shape[0] // RB, top)

    def rest(r, grad):
        g = last[r] + grad
        d_x.ref[r] = g
        d_x.send(r)
        column[0:1] += jnp.sum(g, axis=0, keepdims=True)

    self_back(x_low, proj, out_w, q, k, v, mixed_t, lse, place, length[0], True, grad_low, grad_mixed, d_q, d_k, d_v, pack_a, later, small, rest)
    pair_mark = lax.broadcasted_iota(jnp.int32, (PAIRS, 1), 0) == length[2]
    small[16:] += jnp.where(pair_mark, column[0:1], 0.0)


def dec_self_back(scalars, picks, s, count, two, layer, place, saved, prev):
    proj, out_w, bias, w_in, c_in, w_out, c_out, gain, offset = layer
    x_low, q, k, v, mixed_t, lse, normed1, rstd1 = saved
    n, d = x_low.shape
    nd = (n, d)
    args = [(two, ("late", 1)), (normed1, "late"), (two, ("late", 0))]
    args += [(a, "late") for a in (out_w, mixed_t, q, k, v, x_low, proj)]
    args += [(a, "vmem") for a in (lse, rstd1, gain, place)]
    if prev:
        args.append((prev[3], "vmem"))
    outs = [(nd, F32, ("late", s, prev[0] if prev else None, count)), ((4 * d, d), BF, ("from", prev[1]) if prev else "late"), ((16 + PAIRS, d), F32, "vmem")]
    scratch = [(nd, F32)] + [(nd, BF)] * 5 + [((8, d), F32)]
    return call(functools.partial(dec_self_back_kernel, bool(prev)), "decoder_self_back", scalars, picks, args, outs, scratch, 20e9)


def add_rows(target, start, size, sources):
    block = max(b for b in range(16, min(size, 96) + 1, 16) if size % b == 0)

    def body(index):
        here = pl.ds(pl.multiple_of(start + index * block, 16), block)
        value = 0.0
        for ref, begin in sources:
            value = value + ref[pl.ds(pl.multiple_of(begin + index * block, 16), block)].astype(F32)
        target[here] = value.astype(BF)

    loop(size // block, body)


class Ring:
    def __init__(self, count):
        self.m = m = count // 2
        self.me = lax.axis_index("dp")
        self.core = self.me % 2
        chip = self.me // 2
        turn = (chip // 2) * (1 - chip % 2) + (m - 1 - chip // 2) * (chip % 2)
        back = (m - turn) % m
        self.place = turn * (1 - self.core) + back * self.core
        self.place_other = turn * self.core + back * (1 - self.core)
        self.other = self.me + 1 - 2 * self.core
        self.after = self.device(self.place + 1, self.core)
        self.before = self.device(self.place + m - 1, self.core)

    def device(self, place, core):
        m = self.m
        place = place % m
        turn = place * (1 - core) + ((m - place) % m) * core
        odd = turn // (m // 2)
        return 2 * (2 * (turn * (1 - odd) + (m - 1 - turn) * odd) + odd) + core


def rows_of(ref, start, size):
    return ref.at[pl.ds(pl.multiple_of(start, 16), size)]


class Copies:
    def __init__(self, send_sem, recv_sem):
        self.send_sem, self.recv_sem, self.used = send_sem, recv_sem, 0

    def remote(self, src, dst, device):
        index = self.used
        self.used += 1
        return pltpu.make_async_remote_copy(
            src, dst, self.send_sem.at[index], self.recv_sem.at[index], device_id=device, device_id_type=MESH
        )


def halves(size):
    first = size // 32 * 16
    return [(0, first), (first, size - first)] if first else [(0, size)]


def reduce_kernel(count, shares, a, b, own, out, work, inbox, pairbox, load_sem, send_sem, recv_sem):
    ring = Ring(count)
    m, core, place = ring.m, ring.core, ring.place
    section = lax.axis_index("section")
    na, nb, width = a.shape[0], b.shape[0], a.shape[1]
    bases = (0, count * shares[0], count * (shares[0] + shares[1]))
    starts = (0, shares[0], shares[0] + shares[1])
    loads = [
        pltpu.make_async_copy(a, work.at[pl.ds(0, na)], load_sem.at[0]),
        pltpu.make_async_copy(b, work.at[pl.ds(bases[1], nb)], load_sem.at[1]),
    ]
    for copy in loads:
        copy.start()
    barrier = pltpu.get_barrier_semaphore()
    for device in (ring.after, ring.before, ring.other):
        pl.semaphore_signal(barrier, inc=1, device_id={"dp": device}, device_id_type=MESH)
    blank = jnp.zeros((bases[1] - na - 16, width), F32)
    work[na : bases[1]] = jnp.concatenate([own[0:16], blank]).astype(BF)
    blank = jnp.zeros((count * shares[2] - own.shape[0] + 16, width), F32)
    work[bases[2] : bases[2] + count * shares[2]] = jnp.concatenate([own[16:], blank]).astype(BF)
    for copy in loads:
        copy.wait()
    pl.semaphore_wait(barrier, 3)
    copies = Copies(send_sem, recv_sem)
    units = [(region, offset, size) for region in range(3) for offset, size in halves(shares[region])]
    boxes, total = [], 0
    for _, _, size in units:
        boxes.append(total)
        total += size

    def where(region, action):
        if region == 0:
            action()
        else:
            pl.when(section == region - 1)(action)

    pairs = [[None] * 3 for _ in range(m)]
    for t in range(m):
        owner = ring.device(ring.place_other + 2 * m - 1 - t, 1 - core)
        for region in range(3):
            size = shares[region]
            pairs[t][region] = copies.remote(
                rows_of(work, bases[region] + owner * size, size),
                pairbox.at[pl.ds(t * sum(shares) + starts[region], size)],
                {"dp": ring.other},
            )
            where(region, pairs[t][region].start)
    sends = [[None] * len(units) for _ in range(m - 1)]
    for t in range(m):
        owner = ring.device(place + 2 * m - 1 - t, core)
        for region in range(3):
            where(region, pairs[t][region].wait_recv)
        for u, (region, offset, size) in enumerate(units):
            start = bases[region] + owner * shares[region] + offset
            if t < m - 1:
                sends[t][u] = copies.remote(rows_of(work, start, size), inbox.at[pl.ds(t * total + boxes[u], size)], {"dp": ring.after})

            def step(t=t, u=u, region=region, offset=offset, size=size, start=start):
                sources = [(work, start), (pairbox, t * sum(shares) + starts[region] + offset)]
                if t:
                    sends[t - 1][u].wait_recv()
                    sources.append((inbox, (t - 1) * total + boxes[u]))
                if t < m - 1:
                    add_rows(work, start, size, sources)
                    sends[t][u].start()
                else:
                    add_rows(out, starts[region] + offset, size, sources)

            where(region, step)
    for t in range(m):
        for region in range(3):
            where(region, pairs[t][region].wait_send)
    for t in range(m - 1):
        for u, (region, _, _) in enumerate(units):
            where(region, sends[t][u].wait_send)


def reduce_grads(count, shares, a, b, own):
    d = a.shape[1]
    m = count // 2
    width = sum(shares)
    units = sum(len(halves(s)) for s in shares)
    slots = (m - 1) * units + m * 3
    anywhere = pl.BlockSpec(memory_space=pl.ANY)
    inside = pl.BlockSpec(memory_space=pltpu.VMEM)
    return pl.pallas_call(
        functools.partial(reduce_kernel, count, shares),
        name="gradient_reduce",
        out_shape=sds((width, d), BF),
        in_specs=[anywhere] * 2 + [inside],
        out_specs=inside,
        scratch_shapes=[
            vm((count * width, d), BF),
            vm(((m - 1) * width, d), BF),
            vm((m * width, d), BF),
            pltpu.SemaphoreType.DMA((2,)),
            pltpu.SemaphoreType.DMA((slots,)),
            pltpu.SemaphoreType.DMA((slots,)),
        ],
        compiler_params=pltpu.CompilerParams(collective_id=0, has_side_effects=True, vmem_limit_bytes=48 * 2**20),
    )(a, b, own)


def gather_kernel(count, shares, mine, theirs, own, out, final, out_sem, send_sem, recv_sem):
    ring = Ring(count)
    m, core, place = ring.m, ring.core, ring.place
    section = lax.axis_index("section")
    decoder = section == 1
    barrier = pltpu.get_barrier_semaphore()
    for device in (ring.after, ring.before, ring.other):
        pl.semaphore_signal(barrier, inc=1, device_id={"dp": device}, device_id_type=MESH)
    pl.semaphore_signal(barrier, inc=1, device_id={"section": 1 - section}, device_id_type=MESH)
    bases = [0]
    for share in shares:
        bases.append(bases[-1] + count * share)
    s0, s1, s2, s3 = shares

    def low(region, place, core):
        return bases[region] + ring.device(place, core) * shares[region]

    def here(region):
        return pl.ds(pl.multiple_of(low(region, place, core), 16), shares[region])

    final[here(0)] = own[0:s0]
    final[here(2)] = (mine[s1:].astype(F32) + theirs[s1:].astype(F32)).astype(BF)

    @pl.when(decoder)
    def _():
        final[here(1)] = (mine[0:s1].astype(F32) + theirs[0:s1].astype(F32)).astype(BF)
        final[here(3)] = own[s0 + s1 :]

    @pl.when(section == 0)
    def _():
        final[here(1)] = own[s0 : s0 + s1]

    pl.semaphore_wait(barrier, 4)
    copies = Copies(send_sem, recv_sem)
    pair = rows_of(final, low(3, place, core), s3)
    across = copies.remote(pair, pair, {"section": 1 - section})
    pl.when(decoder)(across.start)
    passes = [[None] * 4 for _ in range(m - 1)]
    shared = []

    def keep(start, size):
        rows = pl.ds(pl.multiple_of(start, 16), size)
        pltpu.make_async_copy(final.at[rows], out.at[rows], out_sem.at[0]).start()

    for s in range(m):
        for region in range(4):
            block = rows_of(final, low(region, place + 2 * m - s, core), shares[region])
            if s:
                passes[s - 1][region].wait_recv()
            elif region == 3:
                pl.when(section == 0)(across.wait_recv)
            if s < m - 1:
                passes[s][region] = copies.remote(block, block, {"dp": ring.after})
                passes[s][region].start()
            shared.append(copies.remote(block, block, {"dp": ring.other}))
            shared[-1].start()
            keep(low(region, place + 2 * m - s, core), shares[region])
    for s in range(m):
        for region in range(4):
            shared[4 * s + region].wait_recv()
            keep(low(region, ring.place_other + 2 * m - s, 1 - core), shares[region])
    for s in range(m - 1):
        for region in range(4):
            passes[s][region].wait_send()
    for share in shared:
        share.wait_send()
    pl.when(decoder)(across.wait_send)
    pltpu.make_async_copy(final, out, out_sem.at[0]).wait()


def gather_grads(count, shares, mine, theirs, own):
    d = own.shape[1]
    m = count // 2
    rows = count * sum(shares)
    slots = (2 * m - 1) * 4 + 1
    inside = pl.BlockSpec(memory_space=pltpu.VMEM)
    return pl.pallas_call(
        functools.partial(gather_kernel, count, shares),
        name="gradient_gather",
        out_shape=sds((rows, d), BF),
        in_specs=[inside] * 3,
        out_specs=pl.BlockSpec(memory_space=pl.ANY),
        scratch_shapes=[
            vm((rows, d), BF),
            pltpu.SemaphoreType.DMA((1,)),
            pltpu.SemaphoreType.DMA((slots,)),
            pltpu.SemaphoreType.DMA((slots,)),
        ],
        compiler_params=pltpu.CompilerParams(collective_id=1, has_side_effects=True, vmem_limit_bytes=48 * 2**20),
    )(mine, theirs, own)


def unpack_kernel(
    bases, f, pack_ref, shown_e, shown_t, shown_far,
    proj, out_w, bias, w_in, b_in, w_out, b_out, gain, offset, c_proj, c_out, c_bias, c_gain, c_offset, pair, shown,
    pack, f_proj, f_out, f_in, f_w_out, f_cproj, f_cout, rows_shown, in_sem, out_sem, shown_sem,
):
    d = pack_ref.shape[1]
    own_b, own_c, own_p = bases
    section = lax.axis_index("section")
    near = [pltpu.make_async_copy(shown_e, rows_shown, shown_sem.at[0])]
    far = [
        pltpu.make_async_copy(shown_t, rows_shown.at[0], shown_sem.at[0]),
        pltpu.make_async_copy(shown_far, rows_shown.at[1], shown_sem.at[1]),
    ]
    spans = [(0, own_b), (own_b, own_b + f), (own_b + f, own_c), (own_c, pack.shape[0])]
    loads = []
    for i, (begin, end) in enumerate(spans):
        rows = pl.ds(begin, end - begin)
        loads.append(pltpu.make_async_copy(pack_ref.at[rows], pack.at[rows], in_sem.at[i]))
        loads[-1].start()

    @pl.when(section == 0)
    def _():
        near[0].start()

    @pl.when(section == 1)
    def _():
        far[0].start()
        far[1].start()

    leaving = []

    def send(held, out):
        leaving.append(pltpu.make_async_copy(held, out, out_sem.at[len(leaving)]))
        leaving[-1].start()

    loads[0].wait()
    f_proj[...] = pack[0 : 3 * d].astype(F32)
    send(f_proj, proj)
    f_out[...] = pack[3 * d : 4 * d].astype(F32)
    send(f_out, out_w)
    loads[1].wait()
    for c in range(f // d):
        f_in[:, c * d : (c + 1) * d] = pack[own_b + c * d : own_b + (c + 1) * d].astype(F32)
    send(f_in, w_in)
    loads[2].wait()
    f_w_out[...] = pack[own_b + f : own_b + 2 * f].astype(F32)
    send(f_w_out, w_out)
    loads[3].wait()

    @pl.when(section == 0)
    def _():
        near[0].wait()

    @pl.when(section == 1)
    def _():
        far[0].wait()
        far[1].wait()

    send(rows_shown, shown)
    f_cproj[...] = pack[own_c : own_c + 3 * d].astype(F32)
    send(f_cproj, c_proj)
    f_cout[...] = pack[own_c + 3 * d : own_c + 4 * d].astype(F32)
    send(f_cout, c_out)
    small = pack[4 * d : 4 * d + 16].astype(F32)
    middle = pack[own_c + 4 * d : own_c + 4 * d + 16].astype(F32)
    bias[...] = small[0:3]
    row = lax.broadcasted_iota(jnp.int32, (16, 1), 0)
    moved = (section == 1) & (row >= 3) & (row <= 11) & (row != 8) & (row != 10)
    small = jnp.where(moved, middle, small)
    for c in range(f // d):
        b_in[:, c * d : (c + 1) * d] = small[3 + c : 4 + c]
    b_out[...] = small[7:8]
    gain[...] = small[8:10]
    offset[...] = small[10:12]
    c_bias[...] = middle[0:3]
    c_gain[...] = middle[8:9]
    c_offset[...] = middle[10:11]
    pair[...] = pack[own_p : own_p + 16].astype(F32)[0 : pair.shape[0]]
    for copy in leaving:
        copy.wait()


def unpack(pack, bases, f, shown_e, shown_t, shown_far):
    d = pack.shape[1]
    inside = pl.BlockSpec(memory_space=pltpu.VMEM)
    anywhere = pl.BlockSpec(memory_space=pl.ANY)
    shapes = [(3 * d, d), (d, d), (3, d), (d, f), (1, f), (f, d), (1, d), (2, d), (2, d), (3 * d, d), (d, d), (3, d), (1, d), (1, d), (PAIRS, d)]
    large = (0, 1, 3, 5, 9, 10)
    return pl.pallas_call(
        functools.partial(unpack_kernel, bases, f),
        name="unpack",
        out_shape=[sds(s, F32) for s in shapes] + [sds(shown_e.shape, BF)],
        in_specs=[anywhere] * 4,
        out_specs=[anywhere if i in large else inside for i in range(len(shapes))] + [anywhere],
        scratch_shapes=[vm(pack.shape, BF)] + [vm(shapes[i], F32) for i in large]
        + [vm(shown_e.shape, BF), pltpu.SemaphoreType.DMA((4,)), pltpu.SemaphoreType.DMA((7,)), pltpu.SemaphoreType.DMA((2,))],
        compiler_params=pltpu.CompilerParams(vmem_limit_bytes=50 * 2**20),
    )(pack, shown_e, shown_t, shown_far)


def nothing(*refs):
    pass


def blank(*shapes):
    spec = pl.BlockSpec(memory_space=pl.ANY)
    return pl.pallas_call(nothing, name="blank", out_shape=[sds(*s) for s in shapes], out_specs=[spec] * len(shapes))()


def per_device(
    embeds, cotangent, pair_ids, seq_lengths, alive_count,
    self_proj, self_out, self_bias, ffn_in, ffn_in_bias, ffn_out, ffn_out_bias, norm_gain, norm_bias,
    cross_proj, cross_out, cross_bias, cross_norm_gain, cross_norm_bias, pair_embed,
):
    layer = (self_proj[0], self_out[0], self_bias[0], ffn_in[0], ffn_in_bias, ffn_out[0], ffn_out_bias, norm_gain[0], norm_bias[0])
    cross = (cross_proj, cross_out, cross_bias, cross_norm_gain[None], cross_norm_bias[None])
    place = jnp.asarray(place_matrix(), BF)
    section_zero = lax.axis_index("section") == 0
    section_one = lax.axis_index("section") == 1
    devices = lax.axis_size("dp")
    x, cot = embeds[0], cotangent[0]
    count, n, d = x.shape
    f = ffn_in.shape[2]
    live = (jnp.arange(count) < alive_count[0])[None, :]
    numbers = jnp.concatenate([seq_lengths.reshape(-1), jnp.where(live, seq_lengths, 0).reshape(-1), pair_ids])
    src = [(s, 2 * count + s, 4 * count + s) for s in range(count)]
    tgt = [(count + s, 3 * count + s, 4 * count + s) for s in range(count)]
    mid = [(s, 3 * count + s, 4 * count + s) for s in range(count)]
    nd, nf, n1 = (n, d), (n, f), (n, 1)
    ahead, behind, both = [(0, 1)], [(1, 0)], [(0, 1), (1, 0)]

    def move(value, way):
        return lax.ppermute(value, "section", way)

    def pick(received, own):
        return jnp.where(section_zero, received, own)

    part = f // devices
    start = lax.axis_index("dp") * part
    share = jnp.concatenate([
        lax.dynamic_slice_in_dim(ffn_in[0], start, part, 1).T, lax.dynamic_slice_in_dim(ffn_out[0], start, part, 0)
    ])
    vectors = jnp.concatenate([ffn_in_bias[:, i : i + d] for i in range(0, f, d)] + [ffn_out_bias, norm_gain[0], norm_bias[0]])
    x, far_share, far_vectors, x_late, cot_late = lax.optimization_barrier(
        (x, move(share, behind), move(vectors, behind), x[1:], cot[1:])
    )
    far_x = move(x_late, behind)
    far_cot = move(cot_late, behind)
    weights = lax.all_gather(pick(far_share, share), "dp", axis=0, tiled=True)
    vectors = pick(far_vectors, vectors)

    def first(e, t, shown):
        def enc():
            memory, shown_e, q, k, v, mt, lse, na, ra, act, slope, nb, rb = enc_forward(numbers, src[e], x, e, layer, shown)
            return memory, shown_e, q, k, v, mt, lse, ra, na, act, slope, nb, rb

        def dec():
            low, q, k, v, mt, lse, na, ra = dec_self(numbers, tgt[t], x, t, pair_embed, layer)
            shown_e, act, slope, nb, rb = blank(((count, *nd), BF), (nf, BF), (nf, BF), (nd, BF), (n1, F32))
            return na, shown_e, q, k, v, mt, lse, ra, low, act, slope, nb, rb

        return lax.cond(section_zero, enc, dec)

    def last(e, t, saved_e, d_memory, grads, saved_t, prev):
        def enc():
            _, _, q, k, v, mt, lse, ra, na, act, slope, nb, rb = saved_e
            return tuple(enc_back(numbers, src[e], x, e, d_memory, cot, layer, place, (q, k, v, mt, lse, na, ra, act, slope, nb, rb), prev))

        def dec():
            na, _, q, k, v, mt, lse, ra, low, _, _, _, _ = saved_t
            d_x, pack_a, small = dec_self_back(
                numbers, tgt[t], t, count, grads, layer, place, (low, q, k, v, mt, lse, na, ra), prev
            )
            return d_x, pack_a, blank(((2 * f, d), BF))[0], small

        return lax.cond(section_one, dec, enc)

    saved = [first(0, 1, None)]
    swapped = move(saved[0][0], both)
    saved.append(first(1, 0, saved[0][1]))
    shown, two, d_memory, pack = dec_mid(
        numbers, (mid[1], mid[0]), ((far_x, 0), (x, 0)), ((far_cot, 0), (cot, 0)), (swapped, saved[1][0]), (saved[1][0], swapped),
        pair_embed, weights, vectors, cross, place, devices,
    )
    near_d_memory = move(d_memory, behind)
    far_two = move(two, ahead)
    mine = lax.psum_scatter(pack, "dp", scatter_dimension=0, tiled=True)
    grads = last(1, 0, saved[1], d_memory, two, saved[1], ())
    shown_late, pack_a = lax.optimization_barrier((shown, grads[1]))
    grads = (grads[0], pack_a, grads[2], grads[3])
    far_shown = move(shown_late, ahead)
    grads = last(0, 1, saved[0], near_d_memory, far_two, saved[0], grads)
    mine, pack_a = lax.optimization_barrier((mine, grads[1]))
    theirs = move(mine, both)
    shares = (padded(4 * d + 16, devices) // devices, 2 * f // devices, cross_rows(devices, d) // devices, 16)
    own = reduce_grads(devices, (shares[0], shares[1], shares[3]), pack_a, grads[2], grads[3])
    pack = gather_grads(devices, shares, mine, theirs, own)
    bases = [devices * sum(shares[:i]) for i in (1, 2, 3)]
    proj, out_w, bias, w_in, b_in, w_out, b_out, gain, offset, c_proj, c_out, c_bias, c_gain, c_offset, pair, shown = unpack(pack, bases, f, saved[1][1], shown, far_shown)
    return (
        shown[None], grads[0][None], proj.reshape(1, 3, d, d), out_w[None], bias[None], w_in[None], b_in, w_out[None], b_out, gain[None], offset[None],
        c_proj.reshape(3, d, d), c_out, c_bias, c_gain[0], c_offset[0], pair,
    )


def solution(mesh):
    s, r = "section", P()
    in_specs = (
        P(s, "dp"), P(s, "dp"), P("dp"), P(None, "dp"), P("dp"),
        P(s), P(s), P(s), P(s), P(s), P(s), P(s), P(s), P(s), r, r, r, r, r, r,
    )
    out_specs = (P(s, "dp"), P(s, "dp"), P(s), P(s), P(s), P(s), P(s), P(s), P(s), P(s), P(s), r, r, r, r, r, r)
    return jax.shard_map(per_device, mesh=mesh, in_specs=in_specs, out_specs=out_specs, check_vma=False)
```

profile of v0, /device:TPU:1, one launch (start us, length us, event | category | flops | bytes accessed | tf_op | source)
XLA Modules:
  0.0 367.1 jit_solution(10955722681271526818)
XLA Ops:
  7.2 0.0 copy-start.2
  7.2 0.0 copy-start.6
  7.2 0.0 copy-start.5
  7.2 0.0 copy-start.4
  7.2 0.0 copy-start.7
  7.2 0.0 copy-start.3
  7.3 0.0 copy-start.8
  7.3 0.0 copy-start.10
  7.3 0.0 copy-start.9
  7.3 0.0 all-gather.2.cloned.1.call-start
  7.3 0.8 fusion
  8.1 1.5 concatenate.11
  9.7 1.3 collective-permute-start.1
  11.0 0.9 dynamic-slice_bitcast_fusion
  11.9 0.9 constant_dynamic-slice_fusion
  12.8 0.1 copy.41
  13.0 1.3 collective-permute-start
  14.3 2.6 slice_bitcast_fusion
  16.9 0.0 collective-permute-done.1
  16.9 5.5 %collective-permute-done = bf16[256,512]{1,0:T(8,128)(2,1)S(1)} collective-permute-done((bf16[256,512]{1,0:T(8,128)(2,1)S(1)}, bf16[256,512]{1,0:T(8,128)(2,1)S(1)}, u32[]{:S(2)}, u32[]{:S(2)}) %collective-permute-start) | collective-permute-done | bytes 262176 | tf_op jit(solution)/shard_map/ppermute | solution.py:1206
  22.4 0.8 broadcast_select_fusion
  23.2 0.0 all-gather.2.cloned.1.call-update
  23.2 0.0 reduce-scatter.2.cloned.1.call-start
  23.9 0.0 copy-done.7
  23.9 0.1 reshape.54
  24.0 0.1 reshape.55
  24.1 0.0 copy-done.3
  24.1 0.0 copy-done.8
  24.1 0.1 pad_add_fusion.numbers
  24.2 1.3 collective-permute-start.3
  25.4 1.3 collective-permute-start.4
  26.7 0.0 copy-done.2
  26.8 27.2 %conditional.4 = (bf16[1024,512]{1,0:T(8,128)(2,1)}, bf16[2,1024,512]{2,1,0:T(8,128)(2,1)}, bf16[1024,512]{1,0:T(8,128)(2,1)}, bf16[1024,512]{1,0:T(8,128)(2,1)}...) conditional(s32[]{:T(128)} %convert_element_type.8, ...), branch_computations={%region_0.1_spmd, %region_1.2_spmd} | conditional | flops 15000000512 | bytes 20971624 | solution.py:1235
  27.1 26.9 %encoder_forward.2 = (bf16[1024,512]{1,0:T(8,128)(2,1)}, bf16[2,1024,512]{2,1,0:T(8,128)(2,1)}, bf16[1024,512]{1,0:T(8,128)(2,1)}, bf16[1024,512]{1,0:T(8,128)(2...) custom-call(s32[10]{0:T(128)S(1)} %get-tuple-element.262.numbers, ...), custom_call_target="tpu_custom_call" | custom-call | flops 15000000512 | bytes 20971520 | tf_op jit(solution)/shard_map/cond/branch_1_fun/encoder_forward/pallas_call | solution.py:379
  54.1 0.1 collective-permute-start.2
  54.1 0.0 copy-start.11
  54.1 27.3 %conditional.5 = (bf16[1024,512]{1,0:T(8,128)(2,1)}, bf16[2,1024,512]{2,1,0:T(8,128)(2,1)}, bf16[1024,512]{1,0:T(8,128)(2,1)}, bf16[1024,512]{1,0:T(8,128)(2,1)}...) conditional(s32[]{:T(128)} %convert_element_type.8, ...), branch_computations={%region_2.3_spmd, %region_3.4_spmd} | conditional | flops 15000000512 | bytes 20971624 | solution.py:1235
  54.7 26.6 %encoder_forward.3 = (bf16[1024,512]{1,0:T(8,128)(2,1)}, bf16[2,1024,512]{2,1,0:T(8,128)(2,1)}, bf16[1024,512]{1,0:T(8,128)(2,1)}, bf16[1024,512]{1,0:T(8,128)(2...) custom-call(s32[10]{0:T(128)S(1)} %get-tuple-element.307.numbers, ...), custom_call_target="tpu_custom_call", output_to_operand_aliasing={{1}: (11, {})} | custom-call | flops 15000000512 | bytes 20971520 | tf_op jit(solution)/shard_map/cond/branch_1_fun/encoder_forward/pallas_call | solution.py:379
  81.5 0.6 broadcast_select_fusion.1.refs_16_
  82.1 0.0 collective-permute-done.3.refs_8_
  82.1 0.0 collective-permute-done.4.refs_10_
  82.1 12.6 %collective-permute-done.2.refs_0_.refs_4_ = bf16[1024,512]{1,0:T(8,128)(2,1)} collective-permute-done((bf16[1024,512]{1,0:T(8,128)(2,1)}, bf16[1024,512]{1,0:T(8,128)(2,1)}, u32[]{:S(2)}, u32[]{:S(2)}) %collective-permute-start.2) | collective-permute-done | bytes 1048608 | tf_op jit(solution)/shard_map/ppermute | solution.py:1206
  94.8 64.4 %decoder_middle.1 = (bf16[1024,512]{1,0:T(8,128)(2,1)}, bf16[2,1024,512]{2,1,0:T(8,128)(2,1)}, bf16[1024,512]{1,0:T(8,128)(2,1)}, bf16[6400,512]{1,0:T(8,128)(2,1)}) custom-call(s32[10]{0:T(128)S(1)} %pad_add_fusion.numbers, bf16[1024,512]{1,0:T(8,128)(2,1)} %collective-permute-done.2.refs_0_.refs_4_, bf16[1024,512]{1,0:T(8,128)(2,1)} %get-tuple-element.504.refs_1_.refs_3_, ...), custom_call_target="tpu_custom_call" | custom-call | flops 54999998464 | bytes 20971520 | tf_op jit(solution)/shard_map/decoder_middle/pallas_call | solution.py:379
  159.2 0.0 reduce-scatter.2.cloned.1.call-update
  159.2 2.7 collective-permute-start.6
  161.9 1.3 collective-permute-start.5
  163.2 0.0 copy-start
  163.2 43.7 %conditional.6 = ((f32[2,1024,512]{2,1,0:T(8,128)}, bf16[2048,512]{1,0:T(8,128)(2,1)}, bf16[4096,512]{1,0:T(8,128)(2,1)}, f32[32,512]{1,0:T(8,128)S(1)})) conditional(s32[]{:T(128)} %convert_element_type.9, (s32[10]{0:T(128)S(1)}, bf16[2,1024,512]{2,1,0:T(8,128)(2,1)}, bf16[1024,512]{1,0:T(8,128)(2,1)}, bf16[1024,512]{1,0:T(8,128)(2,1)}, ...), branch_computations={%region_5.6_spmd, %region_6.7_spmd} | conditional | flops 35000000512 | bytes 20971560 | solution.py:1249
  163.2 43.3 %encoder_back.2 = (f32[2,1024,512]{2,1,0:T(8,128)}, bf16[2048,512]{1,0:T(8,128)(2,1)}, bf16[4096,512]{1,0:T(8,128)(2,1)}, f32[32,512]{1,0:T(8,128)S(1)}) custom-call(s32[10]{0:T(128)S(1)} %get-tuple-element.332.numbers, bf16[2,1024,512]{2,1,0:T(8,128)(2,1)} %get-tuple-element.333.refs_0_, bf16[1024,512]{1,0:T(8,128)(2,1)} %get-tuple-element.334.refs_1_, ...), custom_call_target="tpu_custom_call" | custom-call | flops 35000000512 | bytes 20971520 | tf_op jit(solution)/shard_map/cond/branch_0_fun/encoder_back/pallas_call | solution.py:379
  206.9 0.0 copy-done
  206.9 2.3 collective-permute-start.8
  209.2 0.0 collective-permute-done.5
  209.2 0.0 collective-permute-done.6
  209.2 47.6 %conditional.7 = (bf16[2048,512]{1,0:T(8,128)(2,1)}, bf16[4096,512]{1,0:T(8,128)(2,1)}, f32[32,512]{1,0:T(8,128)S(1)}, f32[1,2,1024,512]{3,2,1,0:T(8,128)}) conditional(s32[]{:T(128)} %convert_element_type.9, (s32[10]{0:T(128)S(1)}, bf16[2,1024,512]{2,1,0:T(8,128)(2,1)}, bf16[1024,512]{1,0:T(8,128)(2,1)}, bf16[1024,512]{1,0:T(8,128)(2,1)}, ...), branch_computations={%region_7.8_spmd, %region_8.9_spmd} | conditional | flops 35000000512 | bytes 20971552 | solution.py:1249
  213.0 43.4 %encoder_back.3 = (f32[2,1024,512]{2,1,0:T(8,128)}, bf16[2048,512]{1,0:T(8,128)(2,1)}, bf16[4096,512]{1,0:T(8,128)(2,1)}, f32[32,512]{1,0:T(8,128)S(1)}) custom-call(s32[10]{0:T(128)S(1)} %get-tuple-element.371.numbers, bf16[2,1024,512]{2,1,0:T(8,128)(2,1)} %get-tuple-element.372.refs_0_, ...), custom_call_target="tpu_custom_call", output_to_operand_aliasing={{0}: (23, {})} | custom-call | flops 35000000512 | bytes 20971520 | tf_op jit(solution)/shard_map/cond/branch_0_fun/encoder_back/pallas_call | solution.py:379
  256.8 0.0 reduce-scatter.2.cloned.1.call-done.mine
  256.8 0.0 copy-start.1
  256.8 0.1 collective-permute-start.7
  256.9 41.3 %gradient_reduce.1.own = bf16[416,512]{1,0:T(8,128)(2,1)S(1)} custom-call(bf16[2048,512]{1,0:T(8,128)(2,1)} %get-tuple-element.542.a, bf16[4096,512]{1,0:T(8,128)(2,1)} %get-tuple-element.543.b, f32[32,512]{1,0:T(8,128)S(1)} %get-tuple-element.544.own), custom_call_target="tpu_custom_call" | custom-call | tf_op jit(solution)/shard_map/gradient_reduce/pallas_call | solution.py:964
  298.2 0.0 collective-permute-done.7.theirs
  298.2 50.1 %gradient_gather.1.pack_ref = bf16[8960,512]{1,0:T(8,128)(2,1)} custom-call(bf16[400,512]{1,0:T(8,128)(2,1)S(1)} %copy-done.1, bf16[400,512]{1,0:T(8,128)(2,1)S(1)} %collective-permute-done.7.theirs, bf16[416,512]{1,0:T(8,128)(2,1)S(1)} %gradient_reduce.1.own), custom_call_target="tpu_custom_call" | custom-call | tf_op jit(solution)/shard_map/gradient_gather/pallas_call | solution.py:1058
  348.3 0.0 collective-permute-done.8.shown_far
  348.3 11.1 %unpack.1 = (f32[1536,512]{1,0:T(8,128)}, f32[512,512]{1,0:T(8,128)}, f32[3,512]{1,0:T(4,128)S(1)}, f32[512,2048]{1,0:T(8,128)}, f32[1,2048]{1,0:T(1,128)}, /*in...) custom-call(bf16[8960,512]{1,0:T(8,128)(2,1)} %gradient_gather.1.pac, ...), custom_call_target="tpu_custom_call" | custom-call | tf_op jit(solution)/shard_map/unpack/pallas_call | solution.py:1162
  359.4 0.6 copy.42
  (12 shorter events, 0.1 us)
Async XLA Ops:
  7.2 19.6 %copy-start.2 = (f32[1,2048]{1,0:T(1,128)S(1)}, f32[1,2048]{1,0:T(1,128)}, u32[]{:S(2)}) copy-start(f32[1,2048]{1,0:T(1,128)} %param.38) | copy-start | bytes 24580
  7.2 19.6 %copy-start.6 = (f32[1,512]{1,0:T(1,128)S(1)}, f32[1,512]{1,0:T(1,128)}, u32[]{:S(2)}) copy-start(f32[1,512]{1,0:T(1,128)} %param.40) | copy-start | bytes 6148
  7.2 19.6 %copy-start.5 = (f32[1,2,512]{2,1,0:T(2,128)S(1)}, f32[1,2,512]{2,1,0:T(2,128)}, u32[]{:S(2)}) copy-start(f32[1,2,512]{2,1,0:T(2,128)} %param.42) | copy-start | bytes 12292
  7.2 19.6 %copy-start.4 = (f32[1,2,512]{2,1,0:T(2,128)S(1)}, f32[1,2,512]{2,1,0:T(2,128)}, u32[]{:S(2)}) copy-start(f32[1,2,512]{2,1,0:T(2,128)} %param.41) | copy-start | bytes 12292
  7.2 16.6 %copy-start.7 = (s32[2,2]{1,0:T(2,128)S(1)}, s32[2,2]{1,0:T(2,128)}, u32[]{:S(2)}) copy-start(s32[2,2]{1,0:T(2,128)} %param.32) | copy-start | bytes 52
  7.2 16.8 %copy-start.3 = (f32[1,3,512]{2,0,1:T(1,128)S(1)}, f32[1,3,512]{2,0,1:T(1,128)}, u32[]{:S(2)}) copy-start(f32[1,3,512]{2,0,1:T(1,128)} %param.36) | copy-start | bytes 18436
  7.3 16.8 %copy-start.8 = (s32[2]{0:T(128)S(1)}, s32[2]{0:T(128)}, u32[]{:S(2)}) copy-start(s32[2]{0:T(128)} %param.31) | copy-start | bytes 28
  7.3 19.5 %copy-start.10 = (f32[16,512]{1,0:T(8,128)S(1)}, f32[16,512]{1,0:T(8,128)}, u32[]{:S(2)}) copy-start(f32[16,512]{1,0:T(8,128)} %refs_12_.1) | copy-start | bytes 98308
  7.3 19.5 %copy-start.9 = (bf16[1,512,512]{2,1,0:T(8,128)(2,1)S(1)}, bf16[1,512,512]{2,1,0:T(8,128)(2,1)}, u32[]{:S(2)}) copy-start(bf16[1,512,512]{2,1,0:T(8,128)(2,1)} %param.35) | copy-start | bytes 1572868
  7.3 87.5 %all-gather.2.cloned.1.call-start = ((), (), s32[]{:S(2)}) async-start(), calls=%async_computation.1 | async-start | bytes 4456448 | tf_op jit(solution)/shard_map/all_gather | solution.py:1222
  9.7 7.3 %collective-permute-start.1 = (f32[9,512]{1,0:T(8,128)S(1)}, f32[9,512]{1,0:T(8,128)S(1)}, u32[]{:S(2)}, u32[]{:S(2)}) collective-permute-start(f32[9,512]{1,0:T(8,128)S(1)} %concatenate.11), channel_id=1, source_target_pairs={{16,0},{17,1},{18,2},{19,3},{20,4},{21,5},{22,6},{23,7},{24,8},{25... | collective-permute-start | bytes 55304 | tf_op jit(solution)/shard_map/ppermute | solution.py:1206
  13.0 9.4 %collective-permute-start = (bf16[256,512]{1,0:T(8,128)(2,1)S(1)}, bf16[256,512]{1,0:T(8,128)(2,1)S(1)}, u32[]{:S(2)}, u32[]{:S(2)}) collective-permute-start(bf16[256,512]{1,0:T(8,128)(2,1)S(1)} %pad_maximum_fusion), channel_id=1, source_target_pairs={{16,0},{17,1},{18,2},{19,3},{20,4},{21,5},{22,6},{23,7},{24,8},{25... | collective-permute-start | bytes 786440 | tf_op jit(solution)/shard_map/ppermute | solution.py:1206
  23.2 233.6 %reduce-scatter.2.cloned.1.call-start = ((), (), s32[]{:S(2)}) async-start(), calls=%async_computation.2 | async-start | bytes 6963200 | tf_op jit(solution)/shard_map/reduce_scatter | solution.py:1260
  24.2 58.0 %collective-permute-start.3 = (bf16[1,1024,512]{2,1,0:T(8,128)(2,1)}, bf16[1,1024,512]{2,1,0:T(8,128)(2,1)}, u32[]{:S(2)}, u32[]{:S(2)}) collective-permute-start(bf16[1,1024,512]{2,1,0:T(8,128)(2,1)} %get-tuple-element.506), channel_id=1, source_target_pairs={{16,0},{17,1},{18,2},{19,3},{20,4},{21,5},{22,6},{23,7},{24,8},{25... | collective-permute-start | bytes 3145736 | tf_op jit(solution)/shard_map/ppermute | solution.py:1206
  25.4 56.7 %collective-permute-start.4 = (bf16[1,1024,512]{2,1,0:T(8,128)(2,1)S(1)}, bf16[1,1024,512]{2,1,0:T(8,128)(2,1)}, u32[]{:S(2)}, u32[]{:S(2)}) collective-permute-start(bf16[1,1024,512]{2,1,0:T(8,128)(2,1)S(1)} %get-tuple-element.507), channel_id=1, source_target_pairs={{16,0},{17,1},{18,2},{19,3},{20,4},{21,5},{22,6},{23,7},{24,8},{25... | collective-permute-start | bytes 3145736 | tf_op jit(solution)/shard_map/ppermute | solution.py:1206
  54.1 40.7 %collective-permute-start.2 = (bf16[1024,512]{1,0:T(8,128)(2,1)}, bf16[1024,512]{1,0:T(8,128)(2,1)}, u32[]{:S(2)}, u32[]{:S(2)}) collective-permute-start(bf16[1024,512]{1,0:T(8,128)(2,1)} %get-tuple-element.683), channel_id=1, source_target_pairs={{0,16},{16,0},{1,17},{17,1},{2,18},{18,2},{3,19},{19,3},{4,20},{20... | collective-permute-start | bytes 3145736 | tf_op jit(solution)/shard_map/ppermute | solution.py:1206
  54.1 40.6 %copy-start.11 = (bf16[16,512]{1,0:T(8,128)(2,1)S(1)}, bf16[16,512]{1,0:T(8,128)(2,1)}, u32[]{:S(2)}) copy-start(bf16[16,512]{1,0:T(8,128)(2,1)} %constant.21.clone.refs_17_) | copy-start | bytes 49156
  159.2 50.0 %collective-permute-start.6 = (bf16[2,1024,512]{2,1,0:T(8,128)(2,1)}, bf16[2,1024,512]{2,1,0:T(8,128)(2,1)}, u32[]{:S(2)}, u32[]{:S(2)}) collective-permute-start(bf16[2,1024,512]{2,1,0:T(8,128)(2,1)} %get-tuple-element.533), channel_id=1, source_target_pairs={{0,16},{1,17},{2,18},{3,19},{4,20},{5,21},{6,22},{7,23},{8,24},{9,... | collective-permute-start | bytes 6291464 | tf_op jit(solution)/shard_map/ppermute | solution.py:1206
  161.9 47.3 %collective-permute-start.5 = (bf16[1024,512]{1,0:T(8,128)(2,1)}, bf16[1024,512]{1,0:T(8,128)(2,1)}, u32[]{:S(2)}, u32[]{:S(2)}) collective-permute-start(bf16[1024,512]{1,0:T(8,128)(2,1)} %get-tuple-element.510), channel_id=1, source_target_pairs={{16,0},{17,1},{18,2},{19,3},{20,4},{21,5},{22,6},{23,7},{24,8},{25... | collective-permute-start | bytes 3145736 | tf_op jit(solution)/shard_map/ppermute | solution.py:1206
  163.2 43.7 %copy-start = (bf16[1024,512]{1,0:T(8,128)(2,1)S(1)}, bf16[1024,512]{1,0:T(8,128)(2,1)}, u32[]{:S(2)}) copy-start(bf16[1024,512]{1,0:T(8,128)(2,1)} %get-tuple-element.546.shown_t) | copy-start | bytes 3145732
  206.9 141.4 %collective-permute-start.8 = (bf16[1024,512]{1,0:T(8,128)(2,1)S(1)}, bf16[1024,512]{1,0:T(8,128)(2,1)}, u32[]{:S(2)}, u32[]{:S(2)}) collective-permute-start(bf16[1024,512]{1,0:T(8,128)(2,1)S(1)} %copy-done), channel_id=1, source_target_pairs={{0,16},{1,17},{2,18},{3,19},{4,20},{5,21},{6,22},{7,23},{8,24},{9,... | collective-permute-start | bytes 3145736 | tf_op jit(solution)/shard_map/ppermute | solution.py:1206
  256.8 41.4 %copy-start.1 = (bf16[400,512]{1,0:T(8,128)(2,1)S(1)}, bf16[400,512]{1,0:T(8,128)(2,1)}, u32[]{:S(2)}) copy-start(bf16[400,512]{1,0:T(8,128)(2,1)} %reduce-scatter.2.cloned.1.call-done.mine) | copy-start | bytes 1228804
  256.8 41.4 %collective-permute-start.7 = (bf16[400,512]{1,0:T(8,128)(2,1)}, bf16[400,512]{1,0:T(8,128)(2,1)S(1)}, u32[]{:S(2)}, u32[]{:S(2)}) collective-permute-start(bf16[400,512]{1,0:T(8,128)(2,1)} %reduce-scatter.2.cloned.1.call-done.mine), channel_id=1, source_target_pairs={{0,16},{16,0},{1,17},{17,1},{2,18},{18,2},{3,19},{19,3},{4,20},{20... | collective-permute-start | bytes 1228808 | tf_op jit(solution)/shard_map/ppermute | solution.py:1206
Sparse Core Ops, SparseCore 0:
  23.3 52.6 all-gather.1
  159.3 88.6 reduce-scatter.1
where the time goes:
time: 373 us; the launch traced here: 367 us
  Pallas kernels  307 us (82%)
  waiting for transfers between devices  18.2 us (5%)
  between operations  15.3 us (4%)
  starting transfers between devices  11.6 us (3%)
  local copies, waits for them, and re-layouts  7.75 us (2%)
  loops' own time  5.64 us (2%)
    pallas_call x5, Pallas kernels, call(): pl.pallas_call(body, name=name, out_shape=out_shapes, in_specs=[pl.BlockS...  205 us
    pallas_call x1, Pallas kernels, gather_grads(): pl.pallas_call(functools.partial(gather_kernel, count, shares), name='gra...  50.1 us
    pallas_call x1, Pallas kernels, reduce_grads(): pl.pallas_call(functools.partial(reduce_kernel, count, shares), name='gra...  41.3 us
    ppermute x9, waiting for transfers between devices, move(): return lax.ppermute(value, 'section', way)  18.1 us
    ppermute x9, starting transfers between devices, move(): return lax.ppermute(value, 'section', way)  11.5 us
    pallas_call x1, Pallas kernels, unpack(): pl.pallas_call(functools.partial(unpack_kernel, bases, f), name='unpack',...  11.1 us
  transfers between devices with their start and end apart: 11, of which 2 were waited for; matrix products, arithmetic and copies ran while one was open for 1% of the time, Pallas kernels for 63%

commit v1 on v0

--- a/solution.py
+++ b/solution.py
@@ -639,11 +639,41 @@
     return padded(4 * d + 16, count)
 
 
+def dec_cross_kernel(
+    length, normed1, c_proj, memory, c_bias, vectors,
+    q, k, v, mixed_t, lse, v_t,
+):
+    gain, offset = vectors[5:6], vectors[7:8]
+    normed1, c_proj = normed1.get(), c_proj.get()
+
+    def queries(index):
+        r = row_block(index)
+        y = (normed1[r].astype(F32) * gain + offset).astype(BF)
+        q.ref[r] = (dot(y, c_proj[0]) + c_bias[0:1]).astype(BF)
+
+    loop(normed1.shape[0] // RB, queries)
+    q.send()
+    memory = memory.get()
+
+    def keys(index):
+        r = row_block(index)
+        m = memory[r]
+        k.ref[r] = dot(m, c_proj[1]).astype(BF)
+        v.ref[r] = (dot(m, c_proj[2]) + c_bias[1:2]).astype(BF)
+
+    loop(memory.shape[0] // RB, keys)
+    k.send()
+    v.send()
+    v_t[...] = v.ref[...].T
+    mix_forward(q.ref, k.ref, v_t, length[0], False, mixed_t.ref, lse)
+    mixed_t.send()
+
+
 def dec_mid_kernel(
-    share_b, share_c, length, normed1, c_proj, memory, c_out, w_in, w_out, x, cot,
-    pair_table, c_bias, c_gain, c_offset, vectors, place,
+    share_b, share_c, length, normed1, mixed_t, c_out, w_in, w_out, x, cot, q, k, v, c_proj, memory,
+    lse, pair_table, c_bias, c_gain, c_offset, vectors, place,
     shown, two, d_memory, pack,
-    small, last, top, y_low, z_low, q, k, v, v_t, mixed_t, lse, normed2, rstd2, act, slope, grad_low, grad_mixed, d_q, d_k, d_v,
+    small, last, top, y_low, z_low, normed2, rstd2, act, slope, grad_low, grad_mixed, d_q, d_k, d_v,
 ):
     small[...] = jnp.zeros(small.shape, F32)
     grad_last, grad_first = (two.part(i) for i in range(2))
@@ -666,33 +696,13 @@
     def put_c(start, value):
         put_part(start, value, share_c, share_b)
 
-    normed1, c_proj = normed1.get(), c_proj.get()
+    normed1, mixed_t, c_out, w_in, w_out, x, cot = (a.get() for a in (normed1, mixed_t, c_out, w_in, w_out, x, cot))
     count = normed1.shape[0]
-
-    def queries(index):
-        r = row_block(index)
-        y = (normed1[r].astype(F32) * gain[0:1] + offset[0:1]).astype(BF)
-        y_low[r] = y
-        q[r] = (dot(y, c_proj[0]) + c_bias[0:1]).astype(BF)
-
-    loop(count // RB, queries)
-    memory = memory.get()
-    span = memory.shape[0]
-
-    def keys(index):
-        r = row_block(index)
-        m = memory[r]
-        k[r] = dot(m, c_proj[1]).astype(BF)
-        v[r] = (dot(m, c_proj[2]) + c_bias[1:2]).astype(BF)
-
-    loop(span // RB, keys)
-    v_t[...] = v[...].T
-    mix_forward(q, k, v_t, length[0], False, mixed_t, lse)
-    c_out, w_in, w_out, x, cot = c_out.get(), w_in.get(), w_out.get(), x.get(), cot.get()
 
     def forward(index):
         r = row_block(index)
         y = normed1[r].astype(F32) * gain[0:1] + offset[0:1]
+        y_low[r] = y.astype(BF)
         n2, s2 = norm_rows(y + dot(mixed_t[:, r], c_out[...], TN) + c_bias[2:3])
         normed2[r] = n2.astype(BF)
         rstd2[r] = s2
@@ -726,7 +736,10 @@
     ffn_back(grad_last.ref, act, slope, z_low, w_in, w_out, put_b, small, middle, True)
     grad_mixed[...] = dot(grad_low[...], c_out[...], NT).astype(BF)
     put_c(1536, dot(mixed_t[...], grad_low[...]))
+    q, k, v = q.get(), k.get(), v.get()
     mix_back(q, k, v, mixed_t, lse, grad_mixed, place, length[0], False, d_q, d_k, d_v)
+    c_proj, memory = c_proj.get(), memory.get()
+    span = memory.shape[0]
 
     def back(index):
         r = row_block(index)
@@ -753,23 +766,35 @@
     pack.send()
 
 
-def dec_mid(scalars, picks, x, cot, normed1, memory, pair_table, weights, vectors, cross, place, count):
+def dec_mid(scalars, picks, x, cot, normed1, memory, crossed, pair_table, weights, vectors, cross, place, count):
     c_proj, c_out_w, c_bias, c_gain, c_offset = cross
+    q, k, v, mixed_t, lse = crossed
     n, d = normed1[0].shape
     m = memory[0].shape[0]
     f = weights.shape[0] // 2
     nd, md = (n, d), (m, d)
     part = f // count
     share_b, share_c = 2 * f // count, cross_rows(count, d) // count
-    args = [(normed1[0], ("either", None, normed1[1], None)), (c_proj, "late")]
-    args += [(memory[0], ("either", None, memory[1], None)), (c_out_w, "late")]
+    either = lambda pair: (pair[0], ("either", None, pair[1], None))
+    args = [either(normed1), (mixed_t, "late"), (c_out_w, "late")]
     args += [(weights, ("rows", (f, d), [(2 * part * i + part * j, part * i, part) for i in range(count)])) for j in range(2)]
-    args += [(v[0][0], ("either", v[0][1], v[1][0], v[1][1])) for v in (x, cot)]
-    args += [(a, "vmem") for a in (pair_table, c_bias, c_gain, c_offset, vectors, place)]
+    args += [(a[0][0], ("either", a[0][1], a[1][0], a[1][1])) for a in (x, cot)]
+    args += [(a, "late") for a in (q, k, v, c_proj)] + [either(memory)]
+    args += [(a, "vmem") for a in (lse, pair_table, c_bias, c_gain, c_offset, vectors, place)]
     outs = [(nd, BF, "late"), ((2, n, d), BF, "late"), (md, BF, "late"), ((count * (share_b + share_c), d), BF, "late")]
-    scratch = [((16, d), F32), (nd, F32), (nd, F32), (nd, BF), (nd, BF), (nd, BF), (md, BF), (md, BF), ((d, m), BF), ((d, n), BF)]
-    scratch += [((8, 1, n), F32), (nd, BF), ((n, 1), F32), ((n, f), BF), ((n, f), BF), (nd, BF), (nd, BF), (nd, BF), (md, BF), (md, BF)]
-    return call(functools.partial(dec_mid_kernel, share_b, share_c), "decoder_middle", scalars, picks, args, outs, scratch, 55e9)
+    scratch = [((16, d), F32), (nd, F32), (nd, F32), (nd, BF), (nd, BF)]
+    scratch += [(nd, BF), ((n, 1), F32), ((n, f), BF), ((n, f), BF), (nd, BF), (nd, BF), (nd, BF), (md, BF), (md, BF)]
+    return call(functools.partial(dec_mid_kernel, share_b, share_c), "decoder_middle", scalars, picks, args, outs, scratch, 45e9)
+
+
+def dec_cross(scalars, picks, normed1, memory, vectors, cross):
+    c_proj, c_out_w, c_bias, c_gain, c_offset = cross
+    n, d = normed1[0].shape
+    m = memory[0].shape[0]
+    either = lambda pair: (pair[0], ("either", None, pair[1], None))
+    args = [either(normed1), (c_proj, "late"), either(memory), (c_bias, "vmem"), (vectors, "vmem")]
+    outs = [((n, d), BF, "late"), ((m, d), BF, "late"), ((m, d), BF, "late"), ((d, n), BF, "late"), ((8, 1, n), F32, "vmem")]
+    return call(dec_cross_kernel, "decoder_cross", scalars, picks, args, outs, [((d, m), BF)], 11e9)
 
 
 def dec_self_back_kernel(
@@ -912,45 +937,66 @@
         else:
             pl.when(section == region - 1)(action)
 
-    pairs = [[None] * 3 for _ in range(m)]
-    for t in range(m):
-        owner = ring.device(ring.place_other + 2 * m - 1 - t, 1 - core)
+    near, far = m // 2, m - 1 - m // 2
+
+    def order(place):
+        chunks = []
+        for s in range(near):
+            chunks.append(place + near - s)
+            if s < far:
+                chunks.append(place + 2 * m - far + s)
+        return chunks + [place + m]
+
+    pairs = []
+    for t, chunk in enumerate(order(ring.place_other)):
+        owner = ring.device(chunk, 1 - core)
+        row = []
         for region in range(3):
             size = shares[region]
-            pairs[t][region] = copies.remote(
-                rows_of(work, bases[region] + owner * size, size),
-                pairbox.at[pl.ds(t * sum(shares) + starts[region], size)],
-                {"dp": ring.other},
+            row.append(
+                copies.remote(
+                    rows_of(work, bases[region] + owner * size, size),
+                    pairbox.at[pl.ds(t * sum(shares) + starts[region], size)],
+                    {"dp": ring.other},
+                )
             )
-            where(region, pairs[t][region].start)
-    sends = [[None] * len(units) for _ in range(m - 1)]
-    for t in range(m):
-        owner = ring.device(place + 2 * m - 1 - t, core)
+            where(region, row[region].start)
+        pairs.append(row)
+    slots = [(s, way) for s in range(near) for way in range(2) if way == 0 or s < far]
+    box_of = {slot: i for i, slot in enumerate(slots)}
+    sends = {}
+    for t, chunk in enumerate(order(place)):
+        s, way = slots[t] if t < m - 1 else (None, None)
+        owner = ring.device(chunk, core)
         for region in range(3):
             where(region, pairs[t][region].wait_recv)
         for u, (region, offset, size) in enumerate(units):
             start = bases[region] + owner * shares[region] + offset
-            if t < m - 1:
-                sends[t][u] = copies.remote(rows_of(work, start, size), inbox.at[pl.ds(t * total + boxes[u], size)], {"dp": ring.after})
-
-            def step(t=t, u=u, region=region, offset=offset, size=size, start=start):
+            if s is None:
+                before = [(near - 1, 0), (far - 1, 1)] if far else [(near - 1, 0)]
+            else:
+                before = [(s - 1, way)] if s else []
+                target = ring.after if way == 0 else ring.before
+                box = box_of[(s, way)] * total + boxes[u]
+                sends[(s, way, u)] = copies.remote(rows_of(work, start, size), inbox.at[pl.ds(box, size)], {"dp": target})
+
+            def step(t=t, s=s, way=way, u=u, region=region, offset=offset, size=size, start=start, before=before):
                 sources = [(work, start), (pairbox, t * sum(shares) + starts[region] + offset)]
-                if t:
-                    sends[t - 1][u].wait_recv()
-                    sources.append((inbox, (t - 1) * total + boxes[u]))
-                if t < m - 1:
+                for slot in before:
+                    sends[(*slot, u)].wait_recv()
+                    sources.append((inbox, box_of[slot] * total + boxes[u]))
+                if s is None:
+                    add_rows(out, starts[region] + offset, size, sources)
+                else:
                     add_rows(work, start, size, sources)
-                    sends[t][u].start()
-                else:
-                    add_rows(out, starts[region] + offset, size, sources)
+                    sends[(s, way, u)].start()
 
             where(region, step)
-    for t in range(m):
+    for row in pairs:
         for region in range(3):
-            where(region, pairs[t][region].wait_send)
-    for t in range(m - 1):
-        for u, (region, _, _) in enumerate(units):
-            where(region, sends[t][u].wait_send)
+            where(region, row[region].wait_send)
+    for (s, way, u), copy in sends.items():
+        where(units[u][0], copy.wait_send)
 
 
 def reduce_grads(count, shares, a, b, own):
@@ -1016,33 +1062,38 @@
     pair = rows_of(final, low(3, place, core), s3)
     across = copies.remote(pair, pair, {"section": 1 - section})
     pl.when(decoder)(across.start)
-    passes = [[None] * 4 for _ in range(m - 1)]
-    shared = []
+    near, far = m // 2, m - 1 - m // 2
+    passes, shared, arrived = {}, [], []
 
     def keep(start, size):
         rows = pl.ds(pl.multiple_of(start, 16), size)
         pltpu.make_async_copy(final.at[rows], out.at[rows], out_sem.at[0]).start()
 
-    for s in range(m):
-        for region in range(4):
-            block = rows_of(final, low(region, place + 2 * m - s, core), shares[region])
-            if s:
-                passes[s - 1][region].wait_recv()
-            elif region == 3:
-                pl.when(section == 0)(across.wait_recv)
-            if s < m - 1:
-                passes[s][region] = copies.remote(block, block, {"dp": ring.after})
-                passes[s][region].start()
-            shared.append(copies.remote(block, block, {"dp": ring.other}))
-            shared[-1].start()
-            keep(low(region, place + 2 * m - s, core), shares[region])
-    for s in range(m):
-        for region in range(4):
-            shared[4 * s + region].wait_recv()
-            keep(low(region, ring.place_other + 2 * m - s, 1 - core), shares[region])
-    for s in range(m - 1):
-        for region in range(4):
-            passes[s][region].wait_send()
+    for s in range(near + 1):
+        for way in range(2):
+            if (way == 1 and s > far) or (s == 0 and way == 1 and not far):
+                continue
+            shift = 2 * m - s if way == 0 else s
+            limit, target = (near, ring.after) if way == 0 else (far, ring.before)
+            for region in range(4):
+                block = rows_of(final, low(region, place + shift, core), shares[region])
+                if s:
+                    passes[(s - 1, way, region)].wait_recv()
+                elif region == 3 and way == 0:
+                    pl.when(section == 0)(across.wait_recv)
+                if s < limit:
+                    passes[(s, way, region)] = copies.remote(block, block, {"dp": target})
+                    passes[(s, way, region)].start()
+                if s or way == 0:
+                    shared.append(copies.remote(block, block, {"dp": ring.other}))
+                    shared[-1].start()
+                    keep(low(region, place + shift, core), shares[region])
+                    arrived.append((region, shift))
+    for copy, (region, shift) in zip(shared, arrived):
+        copy.wait_recv()
+        keep(low(region, ring.place_other + shift, 1 - core), shares[region])
+    for copy in passes.values():
+        copy.wait_send()
     for share in shared:
         share.wait_send()
     pl.when(decoder)(across.wait_send)
@@ -1079,7 +1130,7 @@
     d = pack_ref.shape[1]
     own_b, own_c, own_p = bases
     section = lax.axis_index("section")
-    near = [pltpu.make_async_copy(shown_e, rows_shown, shown_sem.at[0])]
+    leave = pltpu.make_async_copy(rows_shown, shown, shown_sem.at[0])
     far = [
         pltpu.make_async_copy(shown_t, rows_shown.at[0], shown_sem.at[0]),
         pltpu.make_async_copy(shown_far, rows_shown.at[1], shown_sem.at[1]),
@@ -1090,10 +1141,6 @@
         rows = pl.ds(begin, end - begin)
         loads.append(pltpu.make_async_copy(pack_ref.at[rows], pack.at[rows], in_sem.at[i]))
         loads[-1].start()
-
-    @pl.when(section == 0)
-    def _():
-        near[0].start()
 
     @pl.when(section == 1)
     def _():
@@ -1120,16 +1167,12 @@
     send(f_w_out, w_out)
     loads[3].wait()
 
-    @pl.when(section == 0)
-    def _():
-        near[0].wait()
-
     @pl.when(section == 1)
     def _():
         far[0].wait()
         far[1].wait()
-
-    send(rows_shown, shown)
+        leave.start()
+
     f_cproj[...] = pack[own_c : own_c + 3 * d].astype(F32)
     send(f_cproj, c_proj)
     f_cout[...] = pack[own_c + 3 * d : own_c + 4 * d].astype(F32)
@@ -1151,6 +1194,7 @@
     pair[...] = pack[own_p : own_p + 16].astype(F32)[0 : pair.shape[0]]
     for copy in leaving:
         copy.wait()
+    pl.when(section == 1)(leave.wait)
 
 
 def unpack(pack, bases, f, shown_e, shown_t, shown_far):
@@ -1165,8 +1209,9 @@
         out_shape=[sds(s, F32) for s in shapes] + [sds(shown_e.shape, BF)],
         in_specs=[anywhere] * 4,
         out_specs=[anywhere if i in large else inside for i in range(len(shapes))] + [anywhere],
+        input_output_aliases={1: len(shapes)},
         scratch_shapes=[vm(pack.shape, BF)] + [vm(shapes[i], F32) for i in large]
-        + [vm(shown_e.shape, BF), pltpu.SemaphoreType.DMA((4,)), pltpu.SemaphoreType.DMA((7,)), pltpu.SemaphoreType.DMA((2,))],
+        + [vm(shown_e.shape, BF), pltpu.SemaphoreType.DMA((4,)), pltpu.SemaphoreType.DMA((6,)), pltpu.SemaphoreType.DMA((2,))],
         compiler_params=pltpu.CompilerParams(vmem_limit_bytes=50 * 2**20),
     )(pack, shown_e, shown_t, shown_far)
 
@@ -1218,7 +1263,6 @@
         (x, move(share, behind), move(vectors, behind), x[1:], cot[1:])
     )
     far_x = move(x_late, behind)
-    far_cot = move(cot_late, behind)
     weights = lax.all_gather(pick(far_share, share), "dp", axis=0, tiled=True)
     vectors = pick(far_vectors, vectors)
 
@@ -1250,9 +1294,15 @@
 
     saved = [first(0, 1, None)]
     swapped = move(saved[0][0], both)
+    near_first, cot_late = lax.optimization_barrier((saved[0][0], cot_late))
+    far_cot = move(cot_late, behind)
+    x, far_x = lax.optimization_barrier((x, far_x))
     saved.append(first(1, 0, saved[0][1]))
+    normed = (swapped, saved[1][0])
+    memory = (saved[1][0], swapped)
+    crossed = dec_cross(numbers, (mid[1], mid[0]), normed, memory, vectors, cross)
     shown, two, d_memory, pack = dec_mid(
-        numbers, (mid[1], mid[0]), ((far_x, 0), (x, 0)), ((far_cot, 0), (cot, 0)), (swapped, saved[1][0]), (saved[1][0], swapped),
+        numbers, (mid[1], mid[0]), ((far_x, 0), (x, 0)), ((far_cot, 0), (cot, 0)), normed, memory, crossed,
         pair_embed, weights, vectors, cross, place, devices,
     )
     near_d_memory = move(d_memory, behind)

time: 373 us -> 363 us (0.973)
  waiting for transfers between devices: 18.2 us -> 5.57 us
    ppermute x9, waiting for transfers between devices: 18.1 us -> 5.5 us  [move(): return lax.ppermute(value, 'section', way)]
    pallas_call x5 -> x6, Pallas kernels: 205 us -> 211 us  [call(): pl.pallas_call(body, name=name, out_shape=out_shapes, in_specs=[pl.BlockS...]
  transfers between devices with their start and end apart: 11 -> 11, of which waited for: 2 -> 1; matrix products, arithmetic and copies ran while one was open for 1% -> 2% of each run, Pallas kernels for 63% -> 69%
where the time goes in v1:
time: 363 us; the launch traced here: 357 us
  Pallas kernels  310 us (85%)
  between operations  15.3 us (4%)
  starting transfers between devices  11.6 us (3%)
  local copies, waits for them, and re-layouts  7.75 us (2%)
  loops' own time  5.62 us (2%)
  waiting for transfers between devices  5.57 us (2%)
    pallas_call x6, Pallas kernels, call(): pl.pallas_call(body, name=name, out_shape=out_shapes, in_specs=[pl.BlockS...  211 us
    pallas_call x1, Pallas kernels, gather_grads(): pl.pallas_call(functools.partial(gather_kernel, count, shares), name='gra...  50.3 us
    pallas_call x1, Pallas kernels, reduce_grads(): pl.pallas_call(functools.partial(reduce_kernel, count, shares), name='gra...  40.1 us
    ppermute x9, starting transfers between devices, move(): return lax.ppermute(value, 'section', way)  11.5 us
    pallas_call x1, Pallas kernels, unpack(): pl.pallas_call(functools.partial(unpack_kernel, bases, f), name='unpack',...  8.8 us
  transfers between devices with their start and end apart: 11, of which 1 were waited for; matrix products, arithmetic and copies ran while one was open for 2% of the time, Pallas kernels for 69%

profile of v1, /device:TPU:1, one launch (start us, length us, event | category | flops | bytes accessed | tf_op | source)
XLA Modules:
  0.0 357.4 jit_solution(1333999431691906590)
XLA Ops:
  7.2 0.0 copy-start.2
  7.2 0.0 copy-start.6
  7.2 0.0 copy-start.5
  7.2 0.0 copy-start.4
  7.2 0.0 copy-start.7
  7.2 0.0 copy-start.3
  7.3 0.0 all-gather.2.cloned.1.call-start
  7.3 0.8 fusion
  8.1 1.5 concatenate.11
  9.7 1.3 collective-permute-start.1
  11.0 0.9 dynamic-slice_bitcast_fusion
  11.9 0.9 constant_dynamic-slice_fusion
  12.8 0.1 copy.42
  13.0 1.3 collective-permute-start
  14.3 2.6 slice_bitcast_fusion
  16.9 0.0 collective-permute-done.1
  16.9 5.5 %collective-permute-done = bf16[256,512]{1,0:T(8,128)(2,1)S(1)} collective-permute-done((bf16[256,512]{1,0:T(8,128)(2,1)S(1)}, bf16[256,512]{1,0:T(8,128)(2,1)S(1)}, u32[]{:S(2)}, u32[]{:S(2)}) %collective-permute-start) | collective-permute-done | bytes 262176 | tf_op jit(solution)/shard_map/ppermute | solution.py:1251
  22.4 0.8 broadcast_select_fusion
  23.2 0.0 all-gather.2.cloned.1.call-update
  23.2 0.0 reduce-scatter.2.cloned.1.call-start
  23.9 0.1 reshape.54
  24.0 0.1 reshape.55
  24.1 0.0 copy-done.3
  24.1 0.1 pad_add_fusion.numbers
  24.2 1.3 collective-permute-start.3
  25.4 0.0 copy-done.2
  25.5 0.0 copy-done.6
  25.5 0.0 copy-done.5
  25.5 0.0 copy-done.4
  25.5 0.0 copy-done.10
  25.5 0.0 copy-done.9
  25.5 27.2 %conditional.4 = (bf16[1024,512]{1,0:T(8,128)(2,1)}, bf16[2,1024,512]{2,1,0:T(8,128)(2,1)}, bf16[1024,512]{1,0:T(8,128)(2,1)}, bf16[1024,512]{1,0:T(8,128)(2,1)}...) conditional(s32[]{:T(128)} %convert_element_type.8, ...), branch_computations={%region_0.1_spmd, %region_1.2_spmd} | conditional | flops 15000000512 | bytes 20971624 | solution.py:1279
  25.8 26.9 %encoder_forward.2 = (bf16[1024,512]{1,0:T(8,128)(2,1)}, bf16[2,1024,512]{2,1,0:T(8,128)(2,1)}, bf16[1024,512]{1,0:T(8,128)(2,1)}, bf16[1024,512]{1,0:T(8,128)(2...) custom-call(s32[10]{0:T(128)S(1)} %get-tuple-element.262.numbers, ...), custom_call_target="tpu_custom_call" | custom-call | flops 15000000512 | bytes 20971520 | tf_op jit(solution)/shard_map/cond/branch_1_fun/encoder_forward/pallas_call | solution.py:379
  52.7 0.1 collective-permute-start.2
  52.8 1.3 collective-permute-start.4
  54.1 0.6 broadcast_select_fusion.1.refs_6_.refs_21_
  54.7 0.0 collective-permute-done.3.refs_6_
  54.7 27.4 %conditional.5 = (bf16[1024,512]{1,0:T(8,128)(2,1)}, bf16[2,1024,512]{2,1,0:T(8,128)(2,1)}, bf16[1024,512]{1,0:T(8,128)(2,1)}, bf16[1024,512]{1,0:T(8,128)(2,1)}...) conditional(s32[]{:T(128)} %convert_element_type.8, ...), branch_computations={%region_2.3_spmd, %region_3.4_spmd} | conditional | flops 15000000512 | bytes 20971624 | solution.py:1279
  55.3 26.7 %encoder_forward.3 = (bf16[1024,512]{1,0:T(8,128)(2,1)}, bf16[2,1024,512]{2,1,0:T(8,128)(2,1)}, bf16[1024,512]{1,0:T(8,128)(2,1)}, bf16[1024,512]{1,0:T(8,128)(2...) custom-call(s32[10]{0:T(128)S(1)} %get-tuple-element.307.numbers, ...), custom_call_target="tpu_custom_call", output_to_operand_aliasing={{1}: (11, {})} | custom-call | flops 15000000512 | bytes 20971520 | tf_op jit(solution)/shard_map/cond/branch_1_fun/encoder_forward/pallas_call | solution.py:379
  82.1 0.0 collective-permute-done.2.refs_0_.refs_4_.refs_15_
  82.2 0.0 copy-start.11
  82.2 17.6 %decoder_cross.1 = (bf16[1024,512]{1,0:T(8,128)(2,1)}, bf16[1024,512]{1,0:T(8,128)(2,1)}, bf16[1024,512]{1,0:T(8,128)(2,1)}, bf16[512,1024]{1,0:T(8,128)(2,1)}, f32[8,1,1024]{2,1,0:T(1,128)}) custom-call(s32[10]{0:T(128)S(1)} %pad_add_fusion.numbers, bf16[1024,512]{1,0:T(8,128)(2,1)} %collective-permute-done.2.refs_0_.refs_4_.refs_15_, ...), custom_call_target="tpu_custom_call" | custom-call | flops 11000000512 | bytes 20971520 | tf_op jit(solution)/shard_map/decoder_cross/pallas_call | solution.py:379
  99.8 0.0 collective-permute-done.4.refs_8_
  99.8 0.0 all-gather.2.cloned.1.call-done.refs_4_.refs_5_
  99.8 0.0 copy-done.11
  99.8 52.9 %decoder_middle.1 = (bf16[1024,512]{1,0:T(8,128)(2,1)}, bf16[2,1024,512]{2,1,0:T(8,128)(2,1)}, bf16[1024,512]{1,0:T(8,128)(2,1)}, bf16[6400,512]{1,0:T(8,128)(2,1)}) custom-call(s32[10]{0:T(128)S(1)} %pad_add_fusion.numbers, bf16[1024,512]{1,0:T(8,128)(2,1)} %collective-permute-done.2.refs_0_.refs_4_.refs_15_, ...), custom_call_target="tpu_custom_call" | custom-call | flops 44999999488 | bytes 20971520 | tf_op jit(solution)/shard_map/decoder_middle/pallas_call | solution.py:379
  152.7 0.0 reduce-scatter.2.cloned.1.call-update
  152.7 2.7 collective-permute-start.6
  155.4 1.3 collective-permute-start.5
  156.7 43.8 %conditional.6 = ((f32[2,1024,512]{2,1,0:T(8,128)}, bf16[2048,512]{1,0:T(8,128)(2,1)}, bf16[4096,512]{1,0:T(8,128)(2,1)}, f32[32,512]{1,0:T(8,128)S(1)})) conditional(s32[]{:T(128)} %convert_element_type.9, (s32[10]{0:T(128)S(1)}, bf16[2,1024,512]{2,1,0:T(8,128)(2,1)}, bf16[1024,512]{1,0:T(8,128)(2,1)}, bf16[1024,512]{1,0:T(8,128)(2,1)}, ...), branch_computations={%region_5.6_spmd, %region_6.7_spmd} | conditional | flops 35000000512 | bytes 20971560 | solution.py:1293
  156.7 43.4 %encoder_back.2 = (f32[2,1024,512]{2,1,0:T(8,128)}, bf16[2048,512]{1,0:T(8,128)(2,1)}, bf16[4096,512]{1,0:T(8,128)(2,1)}, f32[32,512]{1,0:T(8,128)S(1)}) custom-call(s32[10]{0:T(128)S(1)} %get-tuple-element.332.numbers, bf16[2,1024,512]{2,1,0:T(8,128)(2,1)} %get-tuple-element.333.refs_0_, bf16[1024,512]{1,0:T(8,128)(2,1)} %get-tuple-element.334.refs_1_, ...), custom_call_target="tpu_custom_call" | custom-call | flops 35000000512 | bytes 20971520 | tf_op jit(solution)/shard_map/cond/branch_0_fun/encoder_back/pallas_call | solution.py:379
  200.6 2.3 collective-permute-start.8
  202.8 0.0 collective-permute-done.5
  202.8 0.0 collective-permute-done.6
  202.8 47.5 %conditional.7 = (bf16[2048,512]{1,0:T(8,128)(2,1)}, bf16[4096,512]{1,0:T(8,128)(2,1)}, f32[32,512]{1,0:T(8,128)S(1)}, f32[1,2,1024,512]{3,2,1,0:T(8,128)}) conditional(s32[]{:T(128)} %convert_element_type.9, (s32[10]{0:T(128)S(1)}, bf16[2,1024,512]{2,1,0:T(8,128)(2,1)}, bf16[1024,512]{1,0:T(8,128)(2,1)}, bf16[1024,512]{1,0:T(8,128)(2,1)}, ...), branch_computations={%region_7.8_spmd, %region_8.9_spmd} | conditional | flops 35000000512 | bytes 20971552 | solution.py:1293
  206.6 43.3 %encoder_back.3 = (f32[2,1024,512]{2,1,0:T(8,128)}, bf16[2048,512]{1,0:T(8,128)(2,1)}, bf16[4096,512]{1,0:T(8,128)(2,1)}, f32[32,512]{1,0:T(8,128)S(1)}) custom-call(s32[10]{0:T(128)S(1)} %get-tuple-element.371.numbers, bf16[2,1024,512]{2,1,0:T(8,128)(2,1)} %get-tuple-element.372.refs_0_, ...), custom_call_target="tpu_custom_call", output_to_operand_aliasing={{0}: (23, {})} | custom-call | flops 35000000512 | bytes 20971520 | tf_op jit(solution)/shard_map/cond/branch_0_fun/encoder_back/pallas_call | solution.py:379
  250.4 0.0 reduce-scatter.2.cloned.1.call-done.mine
  250.4 0.1 collective-permute-start.7
  250.5 40.1 %gradient_reduce.1.own = bf16[416,512]{1,0:T(8,128)(2,1)S(1)} custom-call(bf16[2048,512]{1,0:T(8,128)(2,1)} %get-tuple-element.558.a, bf16[4096,512]{1,0:T(8,128)(2,1)} %get-tuple-element.559.b, f32[32,512]{1,0:T(8,128)S(1)} %get-tuple-element.560.own), custom_call_target="tpu_custom_call" | custom-call | tf_op jit(solution)/shard_map/gradient_reduce/pallas_call | solution.py:1010
  290.6 0.0 collective-permute-done.7.theirs
  290.6 50.3 %gradient_gather.1.pack_ref = bf16[8960,512]{1,0:T(8,128)(2,1)} custom-call(bf16[400,512]{1,0:T(8,128)(2,1)S(1)} %copy-done.1, bf16[400,512]{1,0:T(8,128)(2,1)S(1)} %collective-permute-done.7.theirs, bf16[416,512]{1,0:T(8,128)(2,1)S(1)} %gradient_reduce.1.own), custom_call_target="tpu_custom_call" | custom-call | tf_op jit(solution)/shard_map/gradient_gather/pallas_call | solution.py:1109
  340.9 0.0 collective-permute-done.8.shown_far
  340.9 8.8 %unpack.1 = (f32[1536,512]{1,0:T(8,128)}, f32[512,512]{1,0:T(8,128)}, f32[3,512]{1,0:T(4,128)S(1)}, f32[512,2048]{1,0:T(8,128)}, f32[1,2048]{1,0:T(1,128)}, /*in...) custom-call(bf16[8960,512]{1,0:T(8,128)(2,1)} %gradient_gather.1.pac, ...), custom_call_target="tpu_custom_call", output_to_operand_aliasing={{15}: (1, {})} | custom-call | tf_op jit(solution)/shard_map/unpack/pallas_call | solution.py:1206
  349.7 0.6 copy.43
  (13 shorter events, 0.1 us)
Async XLA Ops:
  7.2 18.3 %copy-start.2 = (f32[1,2048]{1,0:T(1,128)S(1)}, f32[1,2048]{1,0:T(1,128)}, u32[]{:S(2)}) copy-start(f32[1,2048]{1,0:T(1,128)} %param.38) | copy-start | bytes 24580
  7.2 18.3 %copy-start.6 = (f32[1,512]{1,0:T(1,128)S(1)}, f32[1,512]{1,0:T(1,128)}, u32[]{:S(2)}) copy-start(f32[1,512]{1,0:T(1,128)} %param.40) | copy-start | bytes 6148
  7.2 18.3 %copy-start.5 = (f32[1,2,512]{2,1,0:T(2,128)S(1)}, f32[1,2,512]{2,1,0:T(2,128)}, u32[]{:S(2)}) copy-start(f32[1,2,512]{2,1,0:T(2,128)} %param.42) | copy-start | bytes 12292
  7.2 18.3 %copy-start.4 = (f32[1,2,512]{2,1,0:T(2,128)S(1)}, f32[1,2,512]{2,1,0:T(2,128)}, u32[]{:S(2)}) copy-start(f32[1,2,512]{2,1,0:T(2,128)} %param.41) | copy-start | bytes 12292
  7.2 16.6 %copy-start.7 = (s32[2,2]{1,0:T(2,128)S(1)}, s32[2,2]{1,0:T(2,128)}, u32[]{:S(2)}) copy-start(s32[2,2]{1,0:T(2,128)} %param.32) | copy-start | bytes 52
  7.2 16.8 %copy-start.3 = (f32[1,3,512]{2,0,1:T(1,128)S(1)}, f32[1,3,512]{2,0,1:T(1,128)}, u32[]{:S(2)}) copy-start(f32[1,3,512]{2,0,1:T(1,128)} %param.36) | copy-start | bytes 18436
  7.3 16.8 %copy-start.8 = (s32[2]{0:T(128)S(1)}, s32[2]{0:T(128)}, u32[]{:S(2)}) copy-start(s32[2]{0:T(128)} %param.31) | copy-start | bytes 28
  7.3 18.2 %copy-start.10 = (f32[16,512]{1,0:T(8,128)S(1)}, f32[16,512]{1,0:T(8,128)}, u32[]{:S(2)}) copy-start(f32[16,512]{1,0:T(8,128)} %refs_17_.1) | copy-start | bytes 98308
  7.3 18.2 %copy-start.9 = (bf16[1,512,512]{2,1,0:T(8,128)(2,1)S(1)}, bf16[1,512,512]{2,1,0:T(8,128)(2,1)}, u32[]{:S(2)}) copy-start(bf16[1,512,512]{2,1,0:T(8,128)(2,1)} %param.35) | copy-start | bytes 1572868
  7.3 92.5 %all-gather.2.cloned.1.call-start = ((), (), s32[]{:S(2)}) async-start(), calls=%async_computation.1 | async-start | bytes 4456448 | tf_op jit(solution)/shard_map/all_gather | solution.py:1266
  9.7 7.3 %collective-permute-start.1 = (f32[9,512]{1,0:T(8,128)S(1)}, f32[9,512]{1,0:T(8,128)S(1)}, u32[]{:S(2)}, u32[]{:S(2)}) collective-permute-start(f32[9,512]{1,0:T(8,128)S(1)} %concatenate.11), channel_id=1, source_target_pairs={{16,0},{17,1},{18,2},{19,3},{20,4},{21,5},{22,6},{23,7},{24,8},{25... | collective-permute-start | bytes 55304 | tf_op jit(solution)/shard_map/ppermute | solution.py:1251
  13.0 9.4 %collective-permute-start = (bf16[256,512]{1,0:T(8,128)(2,1)S(1)}, bf16[256,512]{1,0:T(8,128)(2,1)S(1)}, u32[]{:S(2)}, u32[]{:S(2)}) collective-permute-start(bf16[256,512]{1,0:T(8,128)(2,1)S(1)} %pad_maximum_fusion), channel_id=1, source_target_pairs={{16,0},{17,1},{18,2},{19,3},{20,4},{21,5},{22,6},{23,7},{24,8},{25... | collective-permute-start | bytes 786440 | tf_op jit(solution)/shard_map/ppermute | solution.py:1251
  23.2 227.2 %reduce-scatter.2.cloned.1.call-start = ((), (), s32[]{:S(2)}) async-start(), calls=%async_computation.2 | async-start | bytes 6963200 | tf_op jit(solution)/shard_map/reduce_scatter | solution.py:1310
  24.2 30.6 %collective-permute-start.3 = (bf16[1,1024,512]{2,1,0:T(8,128)(2,1)}, bf16[1,1024,512]{2,1,0:T(8,128)(2,1)}, u32[]{:S(2)}, u32[]{:S(2)}) collective-permute-start(bf16[1,1024,512]{2,1,0:T(8,128)(2,1)} %get-tuple-element.511), channel_id=1, source_target_pairs={{16,0},{17,1},{18,2},{19,3},{20,4},{21,5},{22,6},{23,7},{24,8},{25... | collective-permute-start | bytes 3145736 | tf_op jit(solution)/shard_map/ppermute | solution.py:1251
  52.7 29.4 %collective-permute-start.2 = (bf16[1024,512]{1,0:T(8,128)(2,1)}, bf16[1024,512]{1,0:T(8,128)(2,1)}, u32[]{:S(2)}, u32[]{:S(2)}) collective-permute-start(bf16[1024,512]{1,0:T(8,128)(2,1)} %get-tuple-element.699), channel_id=1, source_target_pairs={{0,16},{16,0},{1,17},{17,1},{2,18},{18,2},{3,19},{19,3},{4,20},{20... | collective-permute-start | bytes 3145736 | tf_op jit(solution)/shard_map/ppermute | solution.py:1251
  52.8 47.0 %collective-permute-start.4 = (bf16[1,1024,512]{2,1,0:T(8,128)(2,1)S(1)}, bf16[1,1024,512]{2,1,0:T(8,128)(2,1)}, u32[]{:S(2)}, u32[]{:S(2)}) collective-permute-start(bf16[1,1024,512]{2,1,0:T(8,128)(2,1)S(1)} %get-tuple-element.520), channel_id=1, source_target_pairs={{16,0},{17,1},{18,2},{19,3},{20,4},{21,5},{22,6},{23,7},{24,8},{25... | collective-permute-start | bytes 3145736 | tf_op jit(solution)/shard_map/ppermute | solution.py:1251
  82.2 17.7 %copy-start.11 = (bf16[16,512]{1,0:T(8,128)(2,1)S(1)}, bf16[16,512]{1,0:T(8,128)(2,1)}, u32[]{:S(2)}) copy-start(bf16[16,512]{1,0:T(8,128)(2,1)} %constant.21.clone.refs_22_) | copy-start | bytes 49156
  152.7 50.1 %collective-permute-start.6 = (bf16[2,1024,512]{2,1,0:T(8,128)(2,1)}, bf16[2,1024,512]{2,1,0:T(8,128)(2,1)}, u32[]{:S(2)}, u32[]{:S(2)}) collective-permute-start(bf16[2,1024,512]{2,1,0:T(8,128)(2,1)} %get-tuple-element.549), channel_id=1, source_target_pairs={{0,16},{1,17},{2,18},{3,19},{4,20},{5,21},{6,22},{7,23},{8,24},{9,... | collective-permute-start | bytes 6291464 | tf_op jit(solution)/shard_map/ppermute | solution.py:1251
  155.4 47.4 %collective-permute-start.5 = (bf16[1024,512]{1,0:T(8,128)(2,1)}, bf16[1024,512]{1,0:T(8,128)(2,1)}, u32[]{:S(2)}, u32[]{:S(2)}) collective-permute-start(bf16[1024,512]{1,0:T(8,128)(2,1)} %get-tuple-element.526), channel_id=1, source_target_pairs={{16,0},{17,1},{18,2},{19,3},{20,4},{21,5},{22,6},{23,7},{24,8},{25... | collective-permute-start | bytes 3145736 | tf_op jit(solution)/shard_map/ppermute | solution.py:1251
  156.7 43.9 %copy-start = (bf16[1024,512]{1,0:T(8,128)(2,1)S(1)}, bf16[1024,512]{1,0:T(8,128)(2,1)}, u32[]{:S(2)}) copy-start(bf16[1024,512]{1,0:T(8,128)(2,1)} %get-tuple-element.562.shown_t) | copy-start | bytes 3145732
  200.6 140.4 %collective-permute-start.8 = (bf16[1024,512]{1,0:T(8,128)(2,1)S(1)}, bf16[1024,512]{1,0:T(8,128)(2,1)}, u32[]{:S(2)}, u32[]{:S(2)}) collective-permute-start(bf16[1024,512]{1,0:T(8,128)(2,1)S(1)} %copy-done), channel_id=1, source_target_pairs={{0,16},{1,17},{2,18},{3,19},{4,20},{5,21},{6,22},{7,23},{8,24},{9,... | collective-permute-start | bytes 3145736 | tf_op jit(solution)/shard_map/ppermute | solution.py:1251
  250.4 40.2 %copy-start.1 = (bf16[400,512]{1,0:T(8,128)(2,1)S(1)}, bf16[400,512]{1,0:T(8,128)(2,1)}, u32[]{:S(2)}) copy-start(bf16[400,512]{1,0:T(8,128)(2,1)} %reduce-scatter.2.cloned.1.call-done.mine) | copy-start | bytes 1228804
  250.4 40.2 %collective-permute-start.7 = (bf16[400,512]{1,0:T(8,128)(2,1)}, bf16[400,512]{1,0:T(8,128)(2,1)S(1)}, u32[]{:S(2)}, u32[]{:S(2)}) collective-permute-start(bf16[400,512]{1,0:T(8,128)(2,1)} %reduce-scatter.2.cloned.1.call-done.mine), channel_id=1, source_target_pairs={{0,16},{16,0},{1,17},{17,1},{2,18},{18,2},{3,19},{19,3},{4,20},{20... | collective-permute-start | bytes 1228808 | tf_op jit(solution)/shard_map/ppermute | solution.py:1251
Sparse Core Ops, SparseCore 0:
  23.3 52.7 all-gather.1
  152.9 88.1 reduce-scatter.1

commit v2 on v1

--- a/solution.py
+++ b/solution.py
@@ -47,6 +47,10 @@
     return tuple(m.astype(F32) for m in (inside, ones, block, flag))
 
 
+def inside_of(half):
+    return (lax.broadcasted_iota(jnp.int32, (1, 128), 1) // 64) == half
+
+
 def norm_rows(value):
     centre = jnp.mean(value, -1, keepdims=True)
     centred = value - centre
@@ -69,7 +73,13 @@
     return hidden * phi, phi + hidden * (bell * 0.3989422804014327)
 
 
-def key_fill(count, length, ones, block):
+def key_fill(count, length):
+    position = lax.broadcasted_iota(jnp.int32, (count, 128), 0)
+    spare = lax.broadcasted_iota(jnp.int32, (count, 128), 1) % 64
+    return jnp.where((spare < 32) | (position < length), jnp.where(spare < 32, 1.0, 0.0), BLOCKED)
+
+
+def spare_keys(count, length, ones, block):
     position = lax.broadcasted_iota(jnp.int32, (count, 128), 0)
     return ones + jnp.where(position < length, 0.0, BLOCKED) * block
 
@@ -80,7 +90,7 @@
     return jnp.where(key <= query, scores, BLOCKED)
 
 
-def mix_forward(queries, keys, values_t, length, causal, mixed_t, lse):
+def mix_forward(queries, keys, values, length, causal, mixed_t, lse):
     count = queries.shape[0]
     span = keys.shape[0]
     size = min(512 if causal else 1024, count)
@@ -89,13 +99,13 @@
         cols = row_block(index, 128)
         q = queries[:, cols].astype(F32) * 0.125
         k = keys[:, cols].astype(F32)
-        vt = values_t[cols, :].astype(F32)
+        vt = values[:, cols].T.astype(F32)
         lane = lax.broadcasted_iota(jnp.int32, (128, 1), 0)
         qa, ka, va = [], [], []
         for half in range(2):
             inside, ones, block, flag = lanes_of(half)
             qa.append((q * inside + flag).astype(BF))
-            ka.append((k * inside + key_fill(span, length, ones, block)).astype(BF))
+            ka.append((k * inside + spare_keys(span, length, ones, block)).astype(BF))
             va.append(jnp.where((lane // 64) == half, vt, 1.0).astype(BF))
 
         def scores_of(part, half):
@@ -143,13 +153,13 @@
 
 
 def place_matrix():
-    out = np.zeros((16, 512), np.float32)
+    out = np.zeros((16, 256), np.float32)
     for half in range(2):
         other = 64 * (1 - half)
         for piece in range(3):
-            out[half * 4 + piece, half * 128 + other + piece] = 1
-            out[8 + half * 4 + piece, 256 + half * 128 + other + piece] = 1
-        out[half * 4 + 3, half * 128 + other + 32] = 1
+            out[half * 4 + piece, other + piece] = 1
+            out[8 + half * 4 + piece, 128 + other + piece] = 1
+        out[half * 4 + 3, other + 32] = 1
     return out
 
 
@@ -157,6 +167,7 @@
     count = queries.shape[0]
     span = keys.shape[0]
     size = 256 if causal else min(512, count)
+    fill = key_fill(span, length)
 
     def pair(index):
         cols = row_block(index, 128)
@@ -180,11 +191,11 @@
         extra = dot(spread.astype(BF), place[...], TN)
         qa, ka, va, ga = [], [], [], []
         for half in range(2):
-            inside, ones, block, flag = lanes_of(half)
-            qa.append((q * inside + extra[:, half * 128 : half * 128 + 128]).astype(BF))
-            ga.append((g * inside + extra[:, 256 + half * 128 : 384 + half * 128]).astype(BF))
-            ka.append((k * inside + key_fill(span, length, ones, block)).astype(BF))
-            va.append((v * inside + (1.0 - inside)).astype(BF))
+            inside = inside_of(half)
+            qa.append(jnp.where(inside, q, extra[:, 0:128]).astype(BF))
+            ga.append(jnp.where(inside, g, extra[:, 128:256]).astype(BF))
+            ka.append(jnp.where(inside, k, fill).astype(BF))
+            va.append(jnp.where(inside, v, 1.0).astype(BF))
         lane = lax.broadcasted_iota(jnp.int32, (size, 128), 1)
         total_k = [None, None]
         total_v = [None, None]
@@ -443,7 +454,7 @@
         put_rows(2048 + c * 512, dot(act[:, cols], g, TN))
 
 
-def project(count, x_low, proj, bias, q, k, v, v_t):
+def project(count, x_low, proj, bias, q, k, v):
     def body(index):
         r = row_block(index)
         x = x_low(r)
@@ -455,7 +466,6 @@
     q.send()
     k.send()
     v.send()
-    v_t[...] = v.ref[...].T
 
 
 def self_back(x, proj, out_w, q, k, v, mixed_t, lse, place, length, causal, grad_low, grad_mixed, d_q, d_k, d_v, pack, later, small, rest):
@@ -489,11 +499,11 @@
 
 def enc_forward_kernel(
     length, x, proj, out_w, w_in, w_out, bias, c_in, c_out, gain, offset,
-    memory, shown, q, k, v, mixed_t, lse, normed1, rstd1, act, slope, normed2, rstd2, v_t,
+    memory, shown, q, k, v, mixed_t, lse, normed1, rstd1, act, slope, normed2, rstd2,
 ):
     x = x.get()
-    project(x.shape[0], lambda r: x[r], proj.get(), bias, q, k, v, v_t)
-    mix_forward(q.ref, k.ref, v_t, length[0], False, mixed_t.ref, lse)
+    project(x.shape[0], lambda r: x[r], proj.get(), bias, q, k, v)
+    mix_forward(q.ref, k.ref, v.ref, length[0], False, mixed_t.ref, lse)
     mixed_t.send()
     out_w, w_in, w_out = out_w.get(), w_in.get(), w_out.get()
 
@@ -528,7 +538,7 @@
         (nd, BF, "late"), (nd, BF, ("late", s, shown, count)), (nd, BF, "late"), (nd, BF, "late"), (nd, BF, "late"), ((d, n), BF, "late"),
         ((8, 1, n), F32, "vmem"), (nd, BF, "late"), ((n, 1), F32, "vmem"), ((n, f), BF, "late"), ((n, f), BF, "late"), (nd, BF, "late"), ((n, 1), F32, "vmem"),
     ]
-    return call(enc_forward_kernel, "encoder_forward", scalars, picks, args, outs, [((d, n), BF)], 15e9)
+    return call(enc_forward_kernel, "encoder_forward", scalars, picks, args, outs, [], 15e9)
 
 
 def enc_back_kernel(
@@ -596,7 +606,7 @@
     return call(functools.partial(enc_back_kernel, bool(prev)), "encoder_back", scalars, picks, args, outs, scratch, 35e9)
 
 
-def dec_self_kernel(length, x, proj, out_w, pair_table, bias, gain, offset, x_low, q, k, v, mixed_t, lse, normed1, rstd1, v_t):
+def dec_self_kernel(length, x, proj, out_w, pair_table, bias, gain, offset, x_low, q, k, v, mixed_t, lse, normed1, rstd1):
     x = x.get()
     pair_row = pair_table[pl.ds(length[2], 1)]
 
@@ -605,9 +615,9 @@
         x_low.ref[r] = value
         return value
 
-    project(x.shape[0], low, proj.get(), bias, q, k, v, v_t)
+    project(x.shape[0], low, proj.get(), bias, q, k, v)
     x_low.send()
-    mix_forward(q.ref, k.ref, v_t, length[0], True, mixed_t.ref, lse)
+    mix_forward(q.ref, k.ref, v.ref, length[0], True, mixed_t.ref, lse)
     mixed_t.send()
     out_w = out_w.get()
 
@@ -628,7 +638,7 @@
     args = [(x, ("late", s)), (proj, "late"), (out_w, "late")]
     args += [(v, "vmem") for v in (pair_table, bias, gain, offset)]
     outs = [(nd, BF, "late")] * 4 + [((d, n), BF, "late"), ((8, 1, n), F32, "vmem"), (nd, BF, "late"), ((n, 1), F32, "vmem")]
-    return call(dec_self_kernel, "decoder_self", scalars, picks, args, outs, [((d, n), BF)], 8e9)
+    return call(dec_self_kernel, "decoder_self", scalars, picks, args, outs, [], 8e9)
 
 
 def padded(rows, count):
@@ -636,12 +646,12 @@
 
 
 def cross_rows(count, d):
-    return padded(4 * d + 16, count)
+    return padded(4 * d, count)
 
 
 def dec_cross_kernel(
     length, normed1, c_proj, memory, c_bias, vectors,
-    q, k, v, mixed_t, lse, v_t,
+    q, k, v, mixed_t, lse,
 ):
     gain, offset = vectors[5:6], vectors[7:8]
     normed1, c_proj = normed1.get(), c_proj.get()
@@ -664,8 +674,7 @@
     loop(memory.shape[0] // RB, keys)
     k.send()
     v.send()
-    v_t[...] = v.ref[...].T
-    mix_forward(q.ref, k.ref, v_t, length[0], False, mixed_t.ref, lse)
+    mix_forward(q.ref, k.ref, v.ref, length[0], False, mixed_t.ref, lse)
     mixed_t.send()
 
 
@@ -686,7 +695,7 @@
         while done < value.shape[0]:
             owner, inner = divmod(start + done, share)
             size = min(share - inner, value.shape[0] - done)
-            begin = owner * (share_b + share_c) + shift + inner
+            begin = owner * (share_b + share_c + 16) + shift + inner
             pack.ref[begin : begin + size] = value[done : done + size]
             done += size
 
@@ -761,8 +770,9 @@
     put_c(0, dot(y_low[...], d_q[...], TN))
     put_c(512, dot(m, d_k[...], TN))
     put_c(1024, dot(m, d_v[...], TN))
-    total_c = pack.ref.shape[0] // (share_b + share_c) * share_c
-    put_c(2048, jnp.concatenate([small[...], jnp.zeros((total_c - 2064, 512), F32)]))
+    for owner in range(pack.ref.shape[0] // (share_b + share_c + 16)):
+        begin = owner * (share_b + share_c + 16) + share_b + share_c
+        pack.ref[begin : begin + 16] = (small[...] if owner == 2 else jnp.zeros((16, 512), F32)).astype(BF)
     pack.send()
 
 
@@ -781,7 +791,7 @@
     args += [(a[0][0], ("either", a[0][1], a[1][0], a[1][1])) for a in (x, cot)]
     args += [(a, "late") for a in (q, k, v, c_proj)] + [either(memory)]
     args += [(a, "vmem") for a in (lse, pair_table, c_bias, c_gain, c_offset, vectors, place)]
-    outs = [(nd, BF, "late"), ((2, n, d), BF, "late"), (md, BF, "late"), ((count * (share_b + share_c), d), BF, "late")]
+    outs = [(nd, BF, "late"), ((2, n, d), BF, "late"), (md, BF, "late"), ((count * (share_b + share_c + 16), d), BF, "late")]
     scratch = [((16, d), F32), (nd, F32), (nd, F32), (nd, BF), (nd, BF)]
     scratch += [(nd, BF), ((n, 1), F32), ((n, f), BF), ((n, f), BF), (nd, BF), (nd, BF), (nd, BF), (md, BF), (md, BF)]
     return call(functools.partial(dec_mid_kernel, share_b, share_c), "decoder_middle", scalars, picks, args, outs, scratch, 45e9)
@@ -794,7 +804,7 @@
     either = lambda pair: (pair[0], ("either", None, pair[1], None))
     args = [either(normed1), (c_proj, "late"), either(memory), (c_bias, "vmem"), (vectors, "vmem")]
     outs = [((n, d), BF, "late"), ((m, d), BF, "late"), ((m, d), BF, "late"), ((d, n), BF, "late"), ((8, 1, n), F32, "vmem")]
-    return call(dec_cross_kernel, "decoder_cross", scalars, picks, args, outs, [((d, m), BF)], 11e9)
+    return call(dec_cross_kernel, "decoder_cross", scalars, picks, args, outs, [], 11e9)
 
 
 def dec_self_back_kernel(
@@ -917,10 +927,8 @@
     barrier = pltpu.get_barrier_semaphore()
     for device in (ring.after, ring.before, ring.other):
         pl.semaphore_signal(barrier, inc=1, device_id={"dp": device}, device_id_type=MESH)
-    blank = jnp.zeros((bases[1] - na - 16, width), F32)
-    work[na : bases[1]] = jnp.concatenate([own[0:16], blank]).astype(BF)
-    blank = jnp.zeros((count * shares[2] - own.shape[0] + 16, width), F32)
-    work[bases[2] : bases[2] + count * shares[2]] = jnp.concatenate([own[16:], blank]).astype(BF)
+    blank = jnp.zeros((count * shares[2] - own.shape[0], width), F32)
+    work[bases[2] : bases[2] + count * shares[2]] = jnp.concatenate([own[16:32], own[0:16], blank]).astype(BF)
     for copy in loads:
         copy.wait()
     pl.semaphore_wait(barrier, 3)
@@ -932,10 +940,10 @@
         total += size
 
     def where(region, action):
-        if region == 0:
+        if region == 1:
+            pl.when(section == 0)(action)
+        else:
             action()
-        else:
-            pl.when(section == region - 1)(action)
 
     near, far = m // 2, m - 1 - m // 2
 
@@ -1025,7 +1033,7 @@
     )(a, b, own)
 
 
-def gather_kernel(count, shares, mine, theirs, own, out, final, out_sem, send_sem, recv_sem):
+def gather_kernel(count, shares, mine, theirs, own, shown, out, shown_far, final, out_sem, send_sem, recv_sem):
     ring = Ring(count)
     m, core, place = ring.m, ring.core, ring.place
     section = lax.axis_index("section")
@@ -1038,80 +1046,119 @@
     for share in shares:
         bases.append(bases[-1] + count * share)
     s0, s1, s2, s3 = shares
+    me = ring.me
+    split = s2 % 32 == 0
+    half = s2 // 2 if split else s2
+    near_half = section * half if split else 0
+    far_half = half - near_half
 
     def low(region, place, core):
         return bases[region] + ring.device(place, core) * shares[region]
 
+    def part(region, place, core):
+        start = low(region, place, core)
+        return (start + near_half, half) if region == 2 else (start, shares[region])
+
     def here(region):
         return pl.ds(pl.multiple_of(low(region, place, core), 16), shares[region])
 
     final[here(0)] = own[0:s0]
-    final[here(2)] = (mine[s1:].astype(F32) + theirs[s1:].astype(F32)).astype(BF)
+    final[here(2)] = (mine[s1 : s1 + s2].astype(F32) + theirs[s1 : s1 + s2].astype(F32)).astype(BF)
 
     @pl.when(decoder)
     def _():
         final[here(1)] = (mine[0:s1].astype(F32) + theirs[0:s1].astype(F32)).astype(BF)
-        final[here(3)] = own[s0 + s1 :]
 
     @pl.when(section == 0)
     def _():
         final[here(1)] = own[s0 : s0 + s1]
+
+    @pl.when(me == 2)
+    def _():
+        final[here(3)] = (mine[s1 + s2 :].astype(F32) + theirs[s1 + s2 :].astype(F32)).astype(BF)
+
+    @pl.when((me != 2) & ((me != 0) | decoder))
+    def _():
+        final[here(3)] = own[s0 + s1 :]
 
     pl.semaphore_wait(barrier, 4)
     copies = Copies(send_sem, recv_sem)
     pair = rows_of(final, low(3, place, core), s3)
     across = copies.remote(pair, pair, {"section": 1 - section})
-    pl.when(decoder)(across.start)
+    pl.when(decoder & (me == 0))(across.start)
+    hand = copies.remote(shown, shown_far, {"section": 1 - section})
+    pl.when(section == 0)(hand.start)
     near, far = m // 2, m - 1 - m // 2
-    passes, shared, arrived = {}, [], []
+    passes, shared, arrived, crossed, waiting = {}, [], [], [], []
 
     def keep(start, size):
         rows = pl.ds(pl.multiple_of(start, 16), size)
         pltpu.make_async_copy(final.at[rows], out.at[rows], out_sem.at[0]).start()
 
+    def give(start, size, far_start):
+        block = rows_of(final, start, size)
+        shared.append(copies.remote(block, block, {"dp": ring.other}))
+        shared[-1].start()
+        keep(start, size)
+        arrived.append((far_start, size))
+
+    def take_crossed():
+        while waiting:
+            copy, shift = waiting.pop(0)
+            copy.wait_recv()
+            give(low(2, place + shift, core) + far_half, half, low(2, ring.place_other + shift, 1 - core) + far_half)
+
     for s in range(near + 1):
+        fresh = []
         for way in range(2):
             if (way == 1 and s > far) or (s == 0 and way == 1 and not far):
                 continue
             shift = 2 * m - s if way == 0 else s
             limit, target = (near, ring.after) if way == 0 else (far, ring.before)
             for region in range(4):
-                block = rows_of(final, low(region, place + shift, core), shares[region])
+                start, size = part(region, place + shift, core)
+                block = rows_of(final, start, size)
                 if s:
                     passes[(s - 1, way, region)].wait_recv()
                 elif region == 3 and way == 0:
-                    pl.when(section == 0)(across.wait_recv)
+                    pl.when((section == 0) & (me == 0))(across.wait_recv)
                 if s < limit:
                     passes[(s, way, region)] = copies.remote(block, block, {"dp": target})
                     passes[(s, way, region)].start()
-                if s or way == 0:
-                    shared.append(copies.remote(block, block, {"dp": ring.other}))
-                    shared[-1].start()
-                    keep(low(region, place + shift, core), shares[region])
-                    arrived.append((region, shift))
-    for copy, (region, shift) in zip(shared, arrived):
+                if s:
+                    if region == 2 and split:
+                        crossed.append(copies.remote(block, block, {"section": 1 - section}))
+                        crossed[-1].start()
+                        fresh.append((crossed[-1], shift))
+                    give(start, size, part(region, ring.place_other + shift, 1 - core)[0])
+                elif way == 0:
+                    give(low(region, place, core), shares[region], low(region, ring.place_other, 1 - core))
+        take_crossed()
+        waiting.extend(fresh)
+    take_crossed()
+    for copy, (start, size) in zip(shared, arrived):
         copy.wait_recv()
-        keep(low(region, ring.place_other + shift, 1 - core), shares[region])
-    for copy in passes.values():
+        keep(start, size)
+    for copy in [*passes.values(), *shared, *crossed]:
         copy.wait_send()
-    for share in shared:
-        share.wait_send()
-    pl.when(decoder)(across.wait_send)
+    pl.when(decoder & (me == 0))(across.wait_send)
+    pl.when(section == 0)(hand.wait_send)
+    pl.when(decoder)(hand.wait_recv)
     pltpu.make_async_copy(final, out, out_sem.at[0]).wait()
 
 
-def gather_grads(count, shares, mine, theirs, own):
+def gather_grads(count, shares, mine, theirs, own, shown):
     d = own.shape[1]
     m = count // 2
     rows = count * sum(shares)
-    slots = (2 * m - 1) * 4 + 1
+    slots = (2 * m - 1) * 4 + 2 + 2 * (m - 1)
     inside = pl.BlockSpec(memory_space=pltpu.VMEM)
     return pl.pallas_call(
         functools.partial(gather_kernel, count, shares),
         name="gradient_gather",
-        out_shape=sds((rows, d), BF),
-        in_specs=[inside] * 3,
-        out_specs=pl.BlockSpec(memory_space=pl.ANY),
+        out_shape=[sds((rows, d), BF), sds(shown.shape, BF)],
+        in_specs=[inside] * 3 + [pl.BlockSpec(memory_space=pl.ANY)],
+        out_specs=[pl.BlockSpec(memory_space=pl.ANY)] * 2,
         scratch_shapes=[
             vm((rows, d), BF),
             pltpu.SemaphoreType.DMA((1,)),
@@ -1119,7 +1166,7 @@
             pltpu.SemaphoreType.DMA((slots,)),
         ],
         compiler_params=pltpu.CompilerParams(collective_id=1, has_side_effects=True, vmem_limit_bytes=48 * 2**20),
-    )(mine, theirs, own)
+    )(mine, theirs, own, shown)
 
 
 def unpack_kernel(
@@ -1177,8 +1224,8 @@
     send(f_cproj, c_proj)
     f_cout[...] = pack[own_c + 3 * d : own_c + 4 * d].astype(F32)
     send(f_cout, c_out)
-    small = pack[4 * d : 4 * d + 16].astype(F32)
-    middle = pack[own_c + 4 * d : own_c + 4 * d + 16].astype(F32)
+    small = pack[own_p + 16 : own_p + 32].astype(F32)
+    middle = pack[own_p + 32 : own_p + 48].astype(F32)
     bias[...] = small[0:3]
     row = lax.broadcasted_iota(jnp.int32, (16, 1), 0)
     moved = (section == 1) & (row >= 3) & (row <= 11) & (row != 8) & (row != 10)
@@ -1258,7 +1305,8 @@
     share = jnp.concatenate([
         lax.dynamic_slice_in_dim(ffn_in[0], start, part, 1).T, lax.dynamic_slice_in_dim(ffn_out[0], start, part, 0)
     ])
-    vectors = jnp.concatenate([ffn_in_bias[:, i : i + d] for i in range(0, f, d)] + [ffn_out_bias, norm_gain[0], norm_bias[0]])
+    share, bias_in = lax.optimization_barrier((share, ffn_in_bias))
+    vectors = jnp.concatenate([bias_in[:, i : i + d] for i in range(0, f, d)] + [ffn_out_bias, norm_gain[0], norm_bias[0]])
     x, far_share, far_vectors, x_late, cot_late = lax.optimization_barrier(
         (x, move(share, behind), move(vectors, behind), x[1:], cot[1:])
     )
@@ -1309,15 +1357,12 @@
     far_two = move(two, ahead)
     mine = lax.psum_scatter(pack, "dp", scatter_dimension=0, tiled=True)
     grads = last(1, 0, saved[1], d_memory, two, saved[1], ())
-    shown_late, pack_a = lax.optimization_barrier((shown, grads[1]))
-    grads = (grads[0], pack_a, grads[2], grads[3])
-    far_shown = move(shown_late, ahead)
     grads = last(0, 1, saved[0], near_d_memory, far_two, saved[0], grads)
     mine, pack_a = lax.optimization_barrier((mine, grads[1]))
     theirs = move(mine, both)
-    shares = (padded(4 * d + 16, devices) // devices, 2 * f // devices, cross_rows(devices, d) // devices, 16)
+    shares = (padded(4 * d, devices) // devices, 2 * f // devices, cross_rows(devices, d) // devices, 16)
     own = reduce_grads(devices, (shares[0], shares[1], shares[3]), pack_a, grads[2], grads[3])
-    pack = gather_grads(devices, shares, mine, theirs, own)
+    pack, far_shown = gather_grads(devices, shares, mine, theirs, own, shown)
     bases = [devices * sum(shares[:i]) for i in (1, 2, 3)]
     proj, out_w, bias, w_in, b_in, w_out, b_out, gain, offset, c_proj, c_out, c_bias, c_gain, c_offset, pair, shown = unpack(pack, bases, f, saved[1][1], shown, far_shown)
     return (

time: 363 us -> 356 us (0.981)
  Pallas kernels: 310 us -> 303 us
    pallas_call x1, Pallas kernels: 50.3 us -> 45 us  [gather_grads(): pl.pallas_call(functools.partial(gather_kernel, count, shares), name='gra...]
    ppermute x9 -> x8, starting transfers between devices: 11.5 us -> 9.23 us  [move(): return lax.ppermute(value, 'section', way)]
  transfers between devices with their start and end apart: 11 -> 10, of which waited for: 1 -> 1; matrix products, arithmetic and copies ran while one was open for 2% -> 1% of each run, Pallas kernels for 69% -> 56%
where the time goes in v2:
time: 356 us; the launch traced here: 350 us
  Pallas kernels  303 us (85%)
  between operations  15.3 us (4%)
  starting transfers between devices  9.31 us (3%)
  loops' own time  7.98 us (2%)
  local copies, waits for them, and re-layouts  7.75 us (2%)
  waiting for transfers between devices  5.57 us (2%)
    pallas_call x6, Pallas kernels, call(): pl.pallas_call(body, name=name, out_shape=out_shapes, in_specs=[pl.BlockS...  208 us
    pallas_call x1, Pallas kernels, gather_grads(): pl.pallas_call(functools.partial(gather_kernel, count, shares), name='gra...  45 us
    pallas_call x1, Pallas kernels, reduce_grads(): pl.pallas_call(functools.partial(reduce_kernel, count, shares), name='gra...  40.7 us
    ppermute x8, starting transfers between devices, move(): return lax.ppermute(value, 'section', way)  9.23 us
    pallas_call x1, Pallas kernels, unpack(): pl.pallas_call(functools.partial(unpack_kernel, bases, f), name='unpack',...  8.63 us
  transfers between devices with their start and end apart: 10, of which 1 were waited for; matrix products, arithmetic and copies ran while one was open for 1% of the time, Pallas kernels for 56%

profile of v2, /device:TPU:1, one launch (start us, length us, event | category | flops | bytes accessed | tf_op | source)
XLA Modules:
  0.0 350.1 jit_solution(11390200275733074420)
XLA Ops:
  7.2 0.0 copy-start.2
  7.2 0.0 copy-start.6
  7.2 0.0 copy-start.5
  7.2 0.0 copy-start.4
  7.2 0.0 copy-start.7
  7.2 0.0 copy-start.3
  7.3 0.0 copy-start.8
  7.3 0.0 copy-start.10
  7.3 0.0 copy-start.9
  7.3 0.0 all-gather.2.cloned.1.call-start
  7.3 1.0 constant_dynamic-slice_fusion
  8.3 0.1 copy.42
  8.4 0.9 dynamic-slice_bitcast_fusion
  9.4 0.7 fusion
  10.1 1.5 concatenate.11
  11.7 1.3 collective-permute-start.1
  13.0 1.3 collective-permute-start
  14.3 2.6 slice_bitcast_fusion
  16.9 0.0 collective-permute-done.1
  16.9 5.5 %collective-permute-done = bf16[256,512]{1,0:T(8,128)(2,1)S(1)} collective-permute-done((bf16[256,512]{1,0:T(8,128)(2,1)S(1)}, bf16[256,512]{1,0:T(8,128)(2,1)S(1)}, u32[]{:S(2)}, u32[]{:S(2)}) %collective-permute-start) | collective-permute-done | bytes 262176 | tf_op jit(solution)/shard_map/ppermute | solution.py:1298
  22.4 0.7 broadcast_select_fusion
  23.1 0.0 all-gather.2.cloned.1.call-update
  23.2 0.0 reduce-scatter.2.cloned.1.call-start
  23.9 0.0 copy-done.7
  23.9 0.1 reshape.54
  24.0 0.1 reshape.55
  24.0 0.0 copy-done.3
  24.0 0.0 copy-done.8
  24.1 0.1 pad_add_fusion.numbers
  24.1 1.3 collective-permute-start.3
  25.4 0.0 copy-done.2
  25.4 0.0 copy-done.6
  25.4 0.0 copy-done.5
  25.5 27.0 %conditional.4 = (bf16[1024,512]{1,0:T(8,128)(2,1)}, bf16[2,1024,512]{2,1,0:T(8,128)(2,1)}, bf16[1024,512]{1,0:T(8,128)(2,1)}, bf16[1024,512]{1,0:T(8,128)(2,1)}...) conditional(s32[]{:T(128)} %convert_element_type.8, ...), branch_computations={%region_0.1_spmd, %region_1.2_spmd} | conditional | flops 15000000512 | bytes 20971624 | solution.py:1327
  25.8 26.6 %encoder_forward.2 = (bf16[1024,512]{1,0:T(8,128)(2,1)}, bf16[2,1024,512]{2,1,0:T(8,128)(2,1)}, bf16[1024,512]{1,0:T(8,128)(2,1)}, bf16[1024,512]{1,0:T(8,128)(2...) custom-call(s32[10]{0:T(128)S(1)} %get-tuple-element.262.numbers, ...), custom_call_target="tpu_custom_call" | custom-call | flops 15000000512 | bytes 20971520 | tf_op jit(solution)/shard_map/cond/branch_1_fun/encoder_forward/pallas_call | solution.py:390
  52.4 0.1 collective-permute-start.2
  52.5 1.3 collective-permute-start.4
  53.8 0.6 broadcast_select_fusion.1.refs_6_.refs_21_
  54.4 0.0 collective-permute-done.3.refs_6_
  54.4 27.2 %conditional.5 = (bf16[1024,512]{1,0:T(8,128)(2,1)}, bf16[2,1024,512]{2,1,0:T(8,128)(2,1)}, bf16[1024,512]{1,0:T(8,128)(2,1)}, bf16[1024,512]{1,0:T(8,128)(2,1)}...) conditional(s32[]{:T(128)} %convert_element_type.8, ...), branch_computations={%region_2.3_spmd, %region_3.4_spmd} | conditional | flops 15000000512 | bytes 20971624 | solution.py:1327
  55.0 26.5 %encoder_forward.3 = (bf16[1024,512]{1,0:T(8,128)(2,1)}, bf16[2,1024,512]{2,1,0:T(8,128)(2,1)}, bf16[1024,512]{1,0:T(8,128)(2,1)}, bf16[1024,512]{1,0:T(8,128)(2...) custom-call(s32[10]{0:T(128)S(1)} %get-tuple-element.307.numbers, ...), custom_call_target="tpu_custom_call", output_to_operand_aliasing={{1}: (11, {})} | custom-call | flops 15000000512 | bytes 20971520 | tf_op jit(solution)/shard_map/cond/branch_1_fun/encoder_forward/pallas_call | solution.py:390
  81.6 0.0 collective-permute-done.2.refs_0_.refs_4_.refs_15_
  81.6 0.0 copy-start.11
  81.6 17.3 %decoder_cross.1 = (bf16[1024,512]{1,0:T(8,128)(2,1)}, bf16[1024,512]{1,0:T(8,128)(2,1)}, bf16[1024,512]{1,0:T(8,128)(2,1)}, bf16[512,1024]{1,0:T(8,128)(2,1)}, f32[8,1,1024]{2,1,0:T(1,128)}) custom-call(s32[10]{0:T(128)S(1)} %pad_add_fusion.numbers, bf16[1024,512]{1,0:T(8,128)(2,1)} %collective-permute-done.2.refs_0_.refs_4_.refs_15_, ...), custom_call_target="tpu_custom_call" | custom-call | flops 11000000512 | bytes 20971520 | tf_op jit(solution)/shard_map/decoder_cross/pallas_call | solution.py:390
  98.9 0.0 collective-permute-done.4.refs_8_
  99.0 0.0 all-gather.2.cloned.1.call-done.refs_4_.refs_5_
  99.0 52.4 %decoder_middle.1 = (bf16[1024,512]{1,0:T(8,128)(2,1)}, bf16[2,1024,512]{2,1,0:T(8,128)(2,1)}, bf16[1024,512]{1,0:T(8,128)(2,1)}, bf16[6400,512]{1,0:T(8,128)(2,1)}) custom-call(s32[10]{0:T(128)S(1)} %pad_add_fusion.numbers, bf16[1024,512]{1,0:T(8,128)(2,1)} %collective-permute-done.2.refs_0_.refs_4_.refs_15_, ...), custom_call_target="tpu_custom_call" | custom-call | flops 44999999488 | bytes 20971520 | tf_op jit(solution)/shard_map/decoder_middle/pallas_call | solution.py:390
  151.5 0.0 reduce-scatter.2.cloned.1.call-update
  151.5 2.7 collective-permute-start.6
  154.1 1.3 collective-permute-start.5
  155.4 43.1 %conditional.6 = ((f32[2,1024,512]{2,1,0:T(8,128)}, bf16[2048,512]{1,0:T(8,128)(2,1)}, bf16[4096,512]{1,0:T(8,128)(2,1)}, f32[32,512]{1,0:T(8,128)S(1)})) conditional(s32[]{:T(128)} %convert_element_type.9, (s32[10]{0:T(128)S(1)}, bf16[2,1024,512]{2,1,0:T(8,128)(2,1)}, bf16[1024,512]{1,0:T(8,128)(2,1)}, bf16[1024,512]{1,0:T(8,128)(2,1)}, ...), branch_computations={%region_5.6_spmd, %region_6.7_spmd} | conditional | flops 35000000512 | bytes 20971560 | solution.py:1341
  155.4 42.7 %encoder_back.2 = (f32[2,1024,512]{2,1,0:T(8,128)}, bf16[2048,512]{1,0:T(8,128)(2,1)}, bf16[4096,512]{1,0:T(8,128)(2,1)}, f32[32,512]{1,0:T(8,128)S(1)}) custom-call(s32[10]{0:T(128)S(1)} %get-tuple-element.332.numbers, bf16[2,1024,512]{2,1,0:T(8,128)(2,1)} %get-tuple-element.333.refs_0_, bf16[1024,512]{1,0:T(8,128)(2,1)} %get-tuple-element.334.refs_1_, ...), custom_call_target="tpu_custom_call" | custom-call | flops 35000000512 | bytes 20971520 | tf_op jit(solution)/shard_map/cond/branch_0_fun/encoder_back/pallas_call | solution.py:390
  198.5 0.0 collective-permute-done.5
  198.6 0.0 collective-permute-done.6
  198.6 49.3 %conditional.7 = (bf16[2048,512]{1,0:T(8,128)(2,1)}, bf16[4096,512]{1,0:T(8,128)(2,1)}, f32[32,512]{1,0:T(8,128)S(1)}, f32[1,2,1024,512]{3,2,1,0:T(8,128)}) conditional(s32[]{:T(128)} %convert_element_type.9, (s32[10]{0:T(128)S(1)}, bf16[2,1024,512]{2,1,0:T(8,128)(2,1)}, bf16[1024,512]{1,0:T(8,128)(2,1)S(1)}, bf16[1024,512]{1,0:T(8,128)(2,1)}, ...), branch_computations={%region_7.8_spmd, %region_8.9_spmd} | conditional | flops 35000000512 | bytes 20971552 | solution.py:1341
  204.7 42.7 %encoder_back.3 = (f32[2,1024,512]{2,1,0:T(8,128)}, bf16[2048,512]{1,0:T(8,128)(2,1)}, bf16[4096,512]{1,0:T(8,128)(2,1)}, f32[32,512]{1,0:T(8,128)S(1)}) custom-call(s32[10]{0:T(128)S(1)} %get-tuple-element.371.numbers, bf16[2,1024,512]{2,1,0:T(8,128)(2,1)} %get-tuple-element.372.refs_0_, ...), custom_call_target="tpu_custom_call", output_to_operand_aliasing={{0}: (23, {})} | custom-call | flops 35000000512 | bytes 20971520 | tf_op jit(solution)/shard_map/cond/branch_0_fun/encoder_back/pallas_call | solution.py:390
  247.9 0.0 reduce-scatter.2.cloned.1.call-done.mine
  247.9 0.0 copy-start.1
  247.9 0.1 collective-permute-start.7
  248.0 40.7 %gradient_reduce.1.own = bf16[400,512]{1,0:T(8,128)(2,1)S(1)} custom-call(bf16[2048,512]{1,0:T(8,128)(2,1)} %get-tuple-element.560.a, bf16[4096,512]{1,0:T(8,128)(2,1)} %get-tuple-element.561.b, f32[32,512]{1,0:T(8,128)S(1)} %get-tuple-element.562.own), custom_call_target="tpu_custom_call" | custom-call | tf_op jit(solution)/shard_map/gradient_reduce/pallas_call | solution.py:1018
  288.7 0.0 collective-permute-done.7.theirs
  288.8 45.0 %gradient_gather.1 = (bf16[8448,512]{1,0:T(8,128)(2,1)}, bf16[1024,512]{1,0:T(8,128)(2,1)S(1)}) custom-call(bf16[400,512]{1,0:T(8,128)(2,1)S(1)} %copy-done.1, bf16[400,512]{1,0:T(8,128)(2,1)S(1)} %collective-permute-done.7.theirs, bf16[400,512]{1,0:T(8,128)(2,1)S(1)} %gradient_reduce.1.own, bf16[1024,512]{1,0:T(8,128)(2,1)S(1)} %copy-done), custom_call_target="tpu_custom_call" | custom-call | tf_op jit(solution)/shard_map/gradient_gather/pallas_call | solution.py:1156
  333.8 8.6 %unpack.1 = (f32[1536,512]{1,0:T(8,128)}, f32[512,512]{1,0:T(8,128)}, f32[3,512]{1,0:T(4,128)S(1)}, f32[512,2048]{1,0:T(8,128)}, f32[1,2048]{1,0:T(1,128)}, /*in...) custom-call(bf16[8448,512]{1,0:T(8,128)(2,1)} %get-tuple-element.564, ...), custom_call_target="tpu_custom_call", output_to_operand_aliasing={{15}: (1, {})} | custom-call | tf_op jit(solution)/shard_map/unpack/pallas_call | solution.py:1253
  342.4 0.6 copy.43
  (11 shorter events, 0.0 us)
Async XLA Ops:
  7.2 18.2 %copy-start.2 = (f32[1,2048]{1,0:T(1,128)S(1)}, f32[1,2048]{1,0:T(1,128)}, u32[]{:S(2)}) copy-start(f32[1,2048]{1,0:T(1,128)} %param.38) | copy-start | bytes 24580
  7.2 18.2 %copy-start.6 = (f32[1,512]{1,0:T(1,128)S(1)}, f32[1,512]{1,0:T(1,128)}, u32[]{:S(2)}) copy-start(f32[1,512]{1,0:T(1,128)} %param.40) | copy-start | bytes 6148
  7.2 18.2 %copy-start.5 = (f32[1,2,512]{2,1,0:T(2,128)S(1)}, f32[1,2,512]{2,1,0:T(2,128)}, u32[]{:S(2)}) copy-start(f32[1,2,512]{2,1,0:T(2,128)} %param.42) | copy-start | bytes 12292
  7.2 18.2 %copy-start.4 = (f32[1,2,512]{2,1,0:T(2,128)S(1)}, f32[1,2,512]{2,1,0:T(2,128)}, u32[]{:S(2)}) copy-start(f32[1,2,512]{2,1,0:T(2,128)} %param.41) | copy-start | bytes 12292
  7.2 16.6 %copy-start.7 = (s32[2,2]{1,0:T(2,128)S(1)}, s32[2,2]{1,0:T(2,128)}, u32[]{:S(2)}) copy-start(s32[2,2]{1,0:T(2,128)} %param.32) | copy-start | bytes 52
  7.2 16.8 %copy-start.3 = (f32[1,3,512]{2,0,1:T(1,128)S(1)}, f32[1,3,512]{2,0,1:T(1,128)}, u32[]{:S(2)}) copy-start(f32[1,3,512]{2,0,1:T(1,128)} %param.36) | copy-start | bytes 18436
  7.3 16.8 %copy-start.8 = (s32[2]{0:T(128)S(1)}, s32[2]{0:T(128)}, u32[]{:S(2)}) copy-start(s32[2]{0:T(128)} %param.31) | copy-start | bytes 28
  7.3 18.2 %copy-start.10 = (f32[16,512]{1,0:T(8,128)S(1)}, f32[16,512]{1,0:T(8,128)}, u32[]{:S(2)}) copy-start(f32[16,512]{1,0:T(8,128)} %refs_17_.1) | copy-start | bytes 98308
  7.3 18.2 %copy-start.9 = (bf16[1,512,512]{2,1,0:T(8,128)(2,1)S(1)}, bf16[1,512,512]{2,1,0:T(8,128)(2,1)}, u32[]{:S(2)}) copy-start(bf16[1,512,512]{2,1,0:T(8,128)(2,1)} %param.35) | copy-start | bytes 1572868
  7.3 91.7 %all-gather.2.cloned.1.call-start = ((), (), s32[]{:S(2)}) async-start(), calls=%async_computation.1 | async-start | bytes 4456448 | tf_op jit(solution)/shard_map/all_gather | solution.py:1314
  11.7 5.3 %collective-permute-start.1 = (f32[9,512]{1,0:T(8,128)S(1)}, f32[9,512]{1,0:T(8,128)S(1)}, u32[]{:S(2)}, u32[]{:S(2)}) collective-permute-start(f32[9,512]{1,0:T(8,128)S(1)} %concatenate.11), channel_id=1, source_target_pairs={{16,0},{17,1},{18,2},{19,3},{20,4},{21,5},{22,6},{23,7},{24,8},{25... | collective-permute-start | bytes 55304 | tf_op jit(solution)/shard_map/ppermute | solution.py:1298
  13.0 9.4 %collective-permute-start = (bf16[256,512]{1,0:T(8,128)(2,1)S(1)}, bf16[256,512]{1,0:T(8,128)(2,1)S(1)}, u32[]{:S(2)}, u32[]{:S(2)}) collective-permute-start(bf16[256,512]{1,0:T(8,128)(2,1)S(1)} %pad_maximum_fusion), channel_id=1, source_target_pairs={{16,0},{17,1},{18,2},{19,3},{20,4},{21,5},{22,6},{23,7},{24,8},{25... | collective-permute-start | bytes 786440 | tf_op jit(solution)/shard_map/ppermute | solution.py:1298
  23.2 224.7 %reduce-scatter.2.cloned.1.call-start = ((), (), s32[]{:S(2)}) async-start(), calls=%async_computation.2 | async-start | bytes 6963200 | tf_op jit(solution)/shard_map/reduce_scatter | solution.py:1358
  24.1 30.3 %collective-permute-start.3 = (bf16[1,1024,512]{2,1,0:T(8,128)(2,1)}, bf16[1,1024,512]{2,1,0:T(8,128)(2,1)}, u32[]{:S(2)}, u32[]{:S(2)}) collective-permute-start(bf16[1,1024,512]{2,1,0:T(8,128)(2,1)} %get-tuple-element.515), channel_id=1, source_target_pairs={{16,0},{17,1},{18,2},{19,3},{20,4},{21,5},{22,6},{23,7},{24,8},{25... | collective-permute-start | bytes 3145736 | tf_op jit(solution)/shard_map/ppermute | solution.py:1298
  52.4 29.2 %collective-permute-start.2 = (bf16[1024,512]{1,0:T(8,128)(2,1)}, bf16[1024,512]{1,0:T(8,128)(2,1)}, u32[]{:S(2)}, u32[]{:S(2)}) collective-permute-start(bf16[1024,512]{1,0:T(8,128)(2,1)} %get-tuple-element.703), channel_id=1, source_target_pairs={{0,16},{16,0},{1,17},{17,1},{2,18},{18,2},{3,19},{19,3},{4,20},{20... | collective-permute-start | bytes 3145736 | tf_op jit(solution)/shard_map/ppermute | solution.py:1298
  52.5 46.4 %collective-permute-start.4 = (bf16[1,1024,512]{2,1,0:T(8,128)(2,1)S(1)}, bf16[1,1024,512]{2,1,0:T(8,128)(2,1)}, u32[]{:S(2)}, u32[]{:S(2)}) collective-permute-start(bf16[1,1024,512]{2,1,0:T(8,128)(2,1)S(1)} %get-tuple-element.524), channel_id=1, source_target_pairs={{16,0},{17,1},{18,2},{19,3},{20,4},{21,5},{22,6},{23,7},{24,8},{25... | collective-permute-start | bytes 3145736 | tf_op jit(solution)/shard_map/ppermute | solution.py:1298
  81.6 17.4 %copy-start.11 = (bf16[16,256]{1,0:T(8,128)(2,1)S(1)}, bf16[16,256]{1,0:T(8,128)(2,1)}, u32[]{:S(2)}) copy-start(bf16[16,256]{1,0:T(8,128)(2,1)} %constant.21.clone.refs_22_) | copy-start | bytes 24580
  151.5 47.1 %collective-permute-start.6 = (bf16[2,1024,512]{2,1,0:T(8,128)(2,1)}, bf16[2,1024,512]{2,1,0:T(8,128)(2,1)}, u32[]{:S(2)}, u32[]{:S(2)}) collective-permute-start(bf16[2,1024,512]{2,1,0:T(8,128)(2,1)} %get-tuple-element.553), channel_id=1, source_target_pairs={{0,16},{1,17},{2,18},{3,19},{4,20},{5,21},{6,22},{7,23},{8,24},{9,... | collective-permute-start | bytes 6291464 | tf_op jit(solution)/shard_map/ppermute | solution.py:1298
  154.1 44.4 %collective-permute-start.5 = (bf16[1024,512]{1,0:T(8,128)(2,1)}, bf16[1024,512]{1,0:T(8,128)(2,1)S(1)}, u32[]{:S(2)}, u32[]{:S(2)}) collective-permute-start(bf16[1024,512]{1,0:T(8,128)(2,1)} %get-tuple-element.530), channel_id=1, source_target_pairs={{16,0},{17,1},{18,2},{19,3},{20,4},{21,5},{22,6},{23,7},{24,8},{25... | collective-permute-start | bytes 3145736 | tf_op jit(solution)/shard_map/ppermute | solution.py:1298
  247.9 40.9 %copy-start = (bf16[1024,512]{1,0:T(8,128)(2,1)S(1)}, bf16[1024,512]{1,0:T(8,128)(2,1)}, u32[]{:S(2)}) copy-start(bf16[1024,512]{1,0:T(8,128)(2,1)} %get-tuple-element.563.shown.shown_t) | copy-start | bytes 3145732
  247.9 40.9 %copy-start.1 = (bf16[400,512]{1,0:T(8,128)(2,1)S(1)}, bf16[400,512]{1,0:T(8,128)(2,1)}, u32[]{:S(2)}) copy-start(bf16[400,512]{1,0:T(8,128)(2,1)} %reduce-scatter.2.cloned.1.call-done.mine) | copy-start | bytes 1228804
  247.9 40.8 %collective-permute-start.7 = (bf16[400,512]{1,0:T(8,128)(2,1)}, bf16[400,512]{1,0:T(8,128)(2,1)S(1)}, u32[]{:S(2)}, u32[]{:S(2)}) collective-permute-start(bf16[400,512]{1,0:T(8,128)(2,1)} %reduce-scatter.2.cloned.1.call-done.mine), channel_id=1, source_target_pairs={{0,16},{16,0},{1,17},{17,1},{2,18},{18,2},{3,19},{19,3},{4,20},{20... | collective-permute-start | bytes 1228808 | tf_op jit(solution)/shard_map/ppermute | solution.py:1298
Sparse Core Ops, SparseCore 0:
  23.3 52.8 all-gather.1
  151.6 88.7 reduce-scatter.1

commit v3 on v2

--- a/solution.py
+++ b/solution.py
@@ -1324,7 +1324,7 @@
             shown_e, act, slope, nb, rb = blank(((count, *nd), BF), (nf, BF), (nf, BF), (nd, BF), (n1, F32))
             return na, shown_e, q, k, v, mt, lse, ra, low, act, slope, nb, rb
 
-        return lax.cond(section_zero, enc, dec)
+        return lax.cond(section_zero, enc, dec) if shown is None else lax.cond(section_one, dec, enc)
 
     def last(e, t, saved_e, d_memory, grads, saved_t, prev):
         def enc():
@@ -1338,7 +1338,7 @@
             )
             return d_x, pack_a, blank(((2 * f, d), BF))[0], small
 
-        return lax.cond(section_one, dec, enc)
+        return lax.cond(section_one, dec, enc) if prev else lax.cond(section_zero, enc, dec)
 
     saved = [first(0, 1, None)]
     swapped = move(saved[0][0], both)

time: 356 us -> 355 us (level)
  loops' own time: 7.98 us -> 1.76 us
  Pallas kernels: 303 us -> 307 us
    another operation x4, loops' own time: 7.98 us -> 1.76 us  [the longest x1 0.64 us: last(): lax.cond(section_zero, enc, dec)]
    pallas_call x6, Pallas kernels: 208 us -> 212 us  [call(): pl.pallas_call(body, name=name, out_shape=out_shapes, in_specs=[pl.BlockS...]
  transfers between devices with their start and end apart: 10 -> 10, of which waited for: 1 -> 2; matrix products, arithmetic and copies ran while one was open for 1% -> 1% of each run, Pallas kernels for 56% -> 57%
where the time goes in v3:
time: 355 us; the launch traced here: 349 us
  Pallas kernels  307 us (86%)
  between operations  15.3 us (4%)
  starting transfers between devices  9.31 us (3%)
  local copies, waits for them, and re-layouts  7.75 us (2%)
  waiting for transfers between devices  5.69 us (2%)
    pallas_call x6, Pallas kernels, call(): pl.pallas_call(body, name=name, out_shape=out_shapes, in_specs=[pl.BlockS...  212 us
    pallas_call x1, Pallas kernels, gather_grads(): pl.pallas_call(functools.partial(gather_kernel, count, shares), name='gra...  45.1 us
    pallas_call x1, Pallas kernels, reduce_grads(): pl.pallas_call(functools.partial(reduce_kernel, count, shares), name='gra...  41.2 us
    ppermute x8, starting transfers between devices, move(): return lax.ppermute(value, 'section', way)  9.23 us
    pallas_call x1, Pallas kernels, unpack(): pl.pallas_call(functools.partial(unpack_kernel, bases, f), name='unpack',...  8.63 us
  transfers between devices with their start and end apart: 10, of which 2 were waited for; matrix products, arithmetic and copies ran while one was open for 1% of the time, Pallas kernels for 57%

profile of v3, /device:TPU:1, one launch (start us, length us, event | category | flops | bytes accessed | tf_op | source)
XLA Modules:
  0.0 348.7 jit_solution(13520211637895354299)
XLA Ops:
  7.2 0.0 copy-start.2
  7.2 0.0 copy-start.6
  7.2 0.0 copy-start.5
  7.2 0.0 copy-start.4
  7.2 0.0 copy-start.7
  7.2 0.0 copy-start.3
  7.3 0.0 copy-start.8
  7.3 0.0 copy-start.10
  7.3 0.0 copy-start.9
  7.3 0.0 all-gather.2.cloned.1.call-start
  7.3 1.0 constant_dynamic-slice_fusion
  8.3 0.1 copy.42
  8.4 0.9 dynamic-slice_bitcast_fusion
  9.4 0.7 fusion
  10.1 1.5 concatenate.11
  11.7 1.3 collective-permute-start.1
  13.0 1.3 collective-permute-start
  14.3 2.6 slice_bitcast_fusion
  16.9 0.0 collective-permute-done.1
  16.9 5.5 %collective-permute-done = bf16[256,512]{1,0:T(8,128)(2,1)S(1)} collective-permute-done((bf16[256,512]{1,0:T(8,128)(2,1)S(1)}, bf16[256,512]{1,0:T(8,128)(2,1)S(1)}, u32[]{:S(2)}, u32[]{:S(2)}) %collective-permute-start) | collective-permute-done | bytes 262176 | tf_op jit(solution)/shard_map/ppermute | solution.py:1298
  22.4 0.7 broadcast_select_fusion
  23.1 0.0 all-gather.2.cloned.1.call-update
  23.2 0.0 reduce-scatter.2.cloned.1.call-start
  23.9 0.1 reshape.54
  24.0 0.1 reshape.55
  24.0 0.0 copy-done.3
  24.1 0.1 pad_add_fusion.numbers
  24.1 1.3 collective-permute-start.3
  25.4 0.0 copy-done.2
  25.4 0.0 copy-done.6
  25.4 0.0 copy-done.5
  25.4 0.0 copy-done.4
  25.5 0.0 copy-done.10
  25.5 0.0 copy-done.9
  25.5 27.2 %conditional.4 = (bf16[1024,512]{1,0:T(8,128)(2,1)}, bf16[2,1024,512]{2,1,0:T(8,128)(2,1)}, bf16[1024,512]{1,0:T(8,128)(2,1)}, bf16[1024,512]{1,0:T(8,128)(2,1)}...) conditional(s32[]{:T(128)} %convert_element_type.8, ...), branch_computations={%region_0.1_spmd, %region_1.2_spmd} | conditional | flops 15000000512 | bytes 20971624 | solution.py:1327
  26.0 26.6 %encoder_forward.2 = (bf16[1024,512]{1,0:T(8,128)(2,1)}, bf16[2,1024,512]{2,1,0:T(8,128)(2,1)}, bf16[1024,512]{1,0:T(8,128)(2,1)}, bf16[1024,512]{1,0:T(8,128)(2...) custom-call(s32[10]{0:T(128)S(1)} %get-tuple-element.262.numbers, ...), custom_call_target="tpu_custom_call" | custom-call | flops 15000000512 | bytes 20971520 | tf_op jit(solution)/shard_map/cond/branch_1_fun/encoder_forward/pallas_call | solution.py:390
  52.7 0.1 collective-permute-start.2
  52.8 1.3 collective-permute-start.4
  54.1 0.6 broadcast_select_fusion.1.refs_6_.refs_21_
  54.7 0.0 collective-permute-done.3.refs_6_
  54.7 26.9 %conditional.5 = (bf16[1024,512]{1,0:T(8,128)(2,1)}, bf16[2,1024,512]{2,1,0:T(8,128)(2,1)}, bf16[1024,512]{1,0:T(8,128)(2,1)}, bf16[1024,512]{1,0:T(8,128)(2,1)}...) conditional(s32[]{:T(128)} %convert_element_type.9, ...), branch_computations={%region_2.3_spmd, %region_3.4_spmd} | conditional | flops 15000000512 | bytes 20971624 | solution.py:1327
  54.8 26.5 %encoder_forward.3 = (bf16[1024,512]{1,0:T(8,128)(2,1)}, bf16[2,1024,512]{2,1,0:T(8,128)(2,1)}, bf16[1024,512]{1,0:T(8,128)(2,1)}, bf16[1024,512]{1,0:T(8,128)(2...) custom-call(s32[10]{0:T(128)S(1)} %get-tuple-element.286.numbers, ...), custom_call_target="tpu_custom_call", output_to_operand_aliasing={{1}: (11, {})} | custom-call | flops 15000000512 | bytes 20971520 | tf_op jit(solution)/shard_map/cond/branch_0_fun/encoder_forward/pallas_call | solution.py:390
  81.5 0.0 collective-permute-done.2.refs_0_.refs_4_.refs_15_
  81.5 0.0 copy-start.11
  81.6 17.3 %decoder_cross.1 = (bf16[1024,512]{1,0:T(8,128)(2,1)}, bf16[1024,512]{1,0:T(8,128)(2,1)}, bf16[1024,512]{1,0:T(8,128)(2,1)}, bf16[512,1024]{1,0:T(8,128)(2,1)}, f32[8,1,1024]{2,1,0:T(1,128)}) custom-call(s32[10]{0:T(128)S(1)} %pad_add_fusion.numbers, bf16[1024,512]{1,0:T(8,128)(2,1)} %collective-permute-done.2.refs_0_.refs_4_.refs_15_, ...), custom_call_target="tpu_custom_call" | custom-call | flops 11000000512 | bytes 20971520 | tf_op jit(solution)/shard_map/decoder_cross/pallas_call | solution.py:390
  98.9 0.1 collective-permute-done.4.refs_8_
  99.0 56.4 %decoder_middle.1 = (bf16[1024,512]{1,0:T(8,128)(2,1)}, bf16[2,1024,512]{2,1,0:T(8,128)(2,1)}, bf16[1024,512]{1,0:T(8,128)(2,1)}, bf16[6400,512]{1,0:T(8,128)(2,1)}) custom-call(s32[10]{0:T(128)S(1)} %pad_add_fusion.numbers, bf16[1024,512]{1,0:T(8,128)(2,1)} %collective-permute-done.2.refs_0_.refs_4_.refs_15_, ...), custom_call_target="tpu_custom_call" | custom-call | flops 44999999488 | bytes 20971520 | tf_op jit(solution)/shard_map/decoder_middle/pallas_call | solution.py:390
  155.5 0.0 reduce-scatter.2.cloned.1.call-update
  155.5 2.7 collective-permute-start.6
  158.1 1.3 collective-permute-start.5
  159.4 43.6 %conditional.6 = ((f32[2,1024,512]{2,1,0:T(8,128)}, bf16[2048,512]{1,0:T(8,128)(2,1)}, bf16[4096,512]{1,0:T(8,128)(2,1)}, f32[32,512]{1,0:T(8,128)S(1)})) conditional(s32[]{:T(128)} %convert_element_type.8, (s32[10]{0:T(128)S(1)}, bf16[2,1024,512]{2,1,0:T(8,128)(2,1)}, bf16[1024,512]{1,0:T(8,128)(2,1)}, bf16[512,512]{1,0:T(8,128)(2,1)S(1)}, ...), branch_computations={%region_5.6_spmd, %region_6.7_spmd} | conditional | flops 35000000512 | bytes 20971560 | solution.py:1341
  159.9 42.9 %encoder_back.2 = (f32[2,1024,512]{2,1,0:T(8,128)}, bf16[2048,512]{1,0:T(8,128)(2,1)}, bf16[4096,512]{1,0:T(8,128)(2,1)}, f32[32,512]{1,0:T(8,128)S(1)}) custom-call(s32[10]{0:T(128)S(1)} %get-tuple-element.349.numbers, bf16[2,1024,512]{2,1,0:T(8,128)(2,1)} %get-tuple-element.350.refs_0_, bf16[1024,512]{1,0:T(8,128)(2,1)} %get-tuple-element.351.refs_1_, ...), custom_call_target="tpu_custom_call" | custom-call | flops 35000000512 | bytes 20971520 | tf_op jit(solution)/shard_map/cond/branch_1_fun/encoder_back/pallas_call | solution.py:390
  203.0 0.0 collective-permute-done.5
  203.0 0.0 collective-permute-done.6
  203.0 42.9 %conditional.7 = (bf16[2048,512]{1,0:T(8,128)(2,1)}, bf16[4096,512]{1,0:T(8,128)(2,1)}, f32[32,512]{1,0:T(8,128)S(1)}, f32[1,2,1024,512]{3,2,1,0:T(8,128)}) conditional(s32[]{:T(128)} %convert_element_type.9, (s32[10]{0:T(128)S(1)}, bf16[2,1024,512]{2,1,0:T(8,128)(2,1)}, bf16[1024,512]{1,0:T(8,128)(2,1)S(1)}, bf16[1024,512]{1,0:T(8,128)(2,1)}, ...), branch_computations={%region_7.8_spmd, %region_8.9_spmd} | conditional | flops 35000000512 | bytes 20971552 | solution.py:1341
  203.0 42.7 %encoder_back.3 = (f32[2,1024,512]{2,1,0:T(8,128)}, bf16[2048,512]{1,0:T(8,128)(2,1)}, bf16[4096,512]{1,0:T(8,128)(2,1)}, f32[32,512]{1,0:T(8,128)S(1)}) custom-call(s32[10]{0:T(128)S(1)} %get-tuple-element.371.numbers, bf16[2,1024,512]{2,1,0:T(8,128)(2,1)} %get-tuple-element.372.refs_0_, ...), custom_call_target="tpu_custom_call", output_to_operand_aliasing={{0}: (23, {})} | custom-call | flops 35000000512 | bytes 20971520 | tf_op jit(solution)/shard_map/cond/branch_0_fun/encoder_back/pallas_call | solution.py:390
  245.9 0.0 reduce-scatter.2.cloned.1.call-done.mine
  246.0 0.0 copy-start.1
  246.0 0.1 collective-permute-start.7
  246.0 41.2 %gradient_reduce.1.own = bf16[400,512]{1,0:T(8,128)(2,1)S(1)} custom-call(bf16[2048,512]{1,0:T(8,128)(2,1)} %get-tuple-element.560.a, bf16[4096,512]{1,0:T(8,128)(2,1)} %get-tuple-element.561.b, f32[32,512]{1,0:T(8,128)S(1)} %get-tuple-element.562.own), custom_call_target="tpu_custom_call" | custom-call | tf_op jit(solution)/shard_map/gradient_reduce/pallas_call | solution.py:1018
  287.3 0.0 collective-permute-done.7.theirs
  287.3 45.1 %gradient_gather.1 = (bf16[8448,512]{1,0:T(8,128)(2,1)}, bf16[1024,512]{1,0:T(8,128)(2,1)S(1)}) custom-call(bf16[400,512]{1,0:T(8,128)(2,1)S(1)} %copy-done.1, bf16[400,512]{1,0:T(8,128)(2,1)S(1)} %collective-permute-done.7.theirs, bf16[400,512]{1,0:T(8,128)(2,1)S(1)} %gradient_reduce.1.own, bf16[1024,512]{1,0:T(8,128)(2,1)S(1)} %copy-done), custom_call_target="tpu_custom_call" | custom-call | tf_op jit(solution)/shard_map/gradient_gather/pallas_call | solution.py:1156
  332.4 8.6 %unpack.1 = (f32[1536,512]{1,0:T(8,128)}, f32[512,512]{1,0:T(8,128)}, f32[3,512]{1,0:T(4,128)S(1)}, f32[512,2048]{1,0:T(8,128)}, f32[1,2048]{1,0:T(1,128)}, /*in...) custom-call(bf16[8448,512]{1,0:T(8,128)(2,1)} %get-tuple-element.564, ...), custom_call_target="tpu_custom_call", output_to_operand_aliasing={{15}: (1, {})} | custom-call | tf_op jit(solution)/shard_map/unpack/pallas_call | solution.py:1253
  341.0 0.6 copy.43
  (11 shorter events, 0.0 us)
Async XLA Ops:
  7.2 18.2 %copy-start.2 = (f32[1,2048]{1,0:T(1,128)S(1)}, f32[1,2048]{1,0:T(1,128)}, u32[]{:S(2)}) copy-start(f32[1,2048]{1,0:T(1,128)} %param.38) | copy-start | bytes 24580
  7.2 18.2 %copy-start.6 = (f32[1,512]{1,0:T(1,128)S(1)}, f32[1,512]{1,0:T(1,128)}, u32[]{:S(2)}) copy-start(f32[1,512]{1,0:T(1,128)} %param.40) | copy-start | bytes 6148
  7.2 18.2 %copy-start.5 = (f32[1,2,512]{2,1,0:T(2,128)S(1)}, f32[1,2,512]{2,1,0:T(2,128)}, u32[]{:S(2)}) copy-start(f32[1,2,512]{2,1,0:T(2,128)} %param.42) | copy-start | bytes 12292
  7.2 18.2 %copy-start.4 = (f32[1,2,512]{2,1,0:T(2,128)S(1)}, f32[1,2,512]{2,1,0:T(2,128)}, u32[]{:S(2)}) copy-start(f32[1,2,512]{2,1,0:T(2,128)} %param.41) | copy-start | bytes 12292
  7.2 16.6 %copy-start.7 = (s32[2,2]{1,0:T(2,128)S(1)}, s32[2,2]{1,0:T(2,128)}, u32[]{:S(2)}) copy-start(s32[2,2]{1,0:T(2,128)} %param.32) | copy-start | bytes 52
  7.2 16.8 %copy-start.3 = (f32[1,3,512]{2,0,1:T(1,128)S(1)}, f32[1,3,512]{2,0,1:T(1,128)}, u32[]{:S(2)}) copy-start(f32[1,3,512]{2,0,1:T(1,128)} %param.36) | copy-start | bytes 18436
  7.3 16.8 %copy-start.8 = (s32[2]{0:T(128)S(1)}, s32[2]{0:T(128)}, u32[]{:S(2)}) copy-start(s32[2]{0:T(128)} %param.31) | copy-start | bytes 28
  7.3 18.2 %copy-start.10 = (f32[16,512]{1,0:T(8,128)S(1)}, f32[16,512]{1,0:T(8,128)}, u32[]{:S(2)}) copy-start(f32[16,512]{1,0:T(8,128)} %refs_17_.1) | copy-start | bytes 98308
  7.3 18.2 %copy-start.9 = (bf16[1,512,512]{2,1,0:T(8,128)(2,1)S(1)}, bf16[1,512,512]{2,1,0:T(8,128)(2,1)}, u32[]{:S(2)}) copy-start(bf16[1,512,512]{2,1,0:T(8,128)(2,1)} %param.35) | copy-start | bytes 1572868
  7.3 91.7 %all-gather.2.cloned.1.call-start = ((), (), s32[]{:S(2)}) async-start(), calls=%async_computation.1 | async-start | bytes 4456448 | tf_op jit(solution)/shard_map/all_gather | solution.py:1314
  11.7 5.3 %collective-permute-start.1 = (f32[9,512]{1,0:T(8,128)S(1)}, f32[9,512]{1,0:T(8,128)S(1)}, u32[]{:S(2)}, u32[]{:S(2)}) collective-permute-start(f32[9,512]{1,0:T(8,128)S(1)} %concatenate.11), channel_id=1, source_target_pairs={{16,0},{17,1},{18,2},{19,3},{20,4},{21,5},{22,6},{23,7},{24,8},{25... | collective-permute-start | bytes 55304 | tf_op jit(solution)/shard_map/ppermute | solution.py:1298
  13.0 9.4 %collective-permute-start = (bf16[256,512]{1,0:T(8,128)(2,1)S(1)}, bf16[256,512]{1,0:T(8,128)(2,1)S(1)}, u32[]{:S(2)}, u32[]{:S(2)}) collective-permute-start(bf16[256,512]{1,0:T(8,128)(2,1)S(1)} %pad_maximum_fusion), channel_id=1, source_target_pairs={{16,0},{17,1},{18,2},{19,3},{20,4},{21,5},{22,6},{23,7},{24,8},{25... | collective-permute-start | bytes 786440 | tf_op jit(solution)/shard_map/ppermute | solution.py:1298
  23.2 222.8 %reduce-scatter.2.cloned.1.call-start = ((), (), s32[]{:S(2)}) async-start(), calls=%async_computation.2 | async-start | bytes 6963200 | tf_op jit(solution)/shard_map/reduce_scatter | solution.py:1358
  24.1 30.6 %collective-permute-start.3 = (bf16[1,1024,512]{2,1,0:T(8,128)(2,1)}, bf16[1,1024,512]{2,1,0:T(8,128)(2,1)}, u32[]{:S(2)}, u32[]{:S(2)}) collective-permute-start(bf16[1,1024,512]{2,1,0:T(8,128)(2,1)} %get-tuple-element.515), channel_id=1, source_target_pairs={{16,0},{17,1},{18,2},{19,3},{20,4},{21,5},{22,6},{23,7},{24,8},{25... | collective-permute-start | bytes 3145736 | tf_op jit(solution)/shard_map/ppermute | solution.py:1298
  52.7 28.9 %collective-permute-start.2 = (bf16[1024,512]{1,0:T(8,128)(2,1)}, bf16[1024,512]{1,0:T(8,128)(2,1)}, u32[]{:S(2)}, u32[]{:S(2)}) collective-permute-start(bf16[1024,512]{1,0:T(8,128)(2,1)} %get-tuple-element.703), channel_id=1, source_target_pairs={{0,16},{16,0},{1,17},{17,1},{2,18},{18,2},{3,19},{19,3},{4,20},{20... | collective-permute-start | bytes 3145736 | tf_op jit(solution)/shard_map/ppermute | solution.py:1298
  52.8 46.3 %collective-permute-start.4 = (bf16[1,1024,512]{2,1,0:T(8,128)(2,1)S(1)}, bf16[1,1024,512]{2,1,0:T(8,128)(2,1)}, u32[]{:S(2)}, u32[]{:S(2)}) collective-permute-start(bf16[1,1024,512]{2,1,0:T(8,128)(2,1)S(1)} %get-tuple-element.524), channel_id=1, source_target_pairs={{16,0},{17,1},{18,2},{19,3},{20,4},{21,5},{22,6},{23,7},{24,8},{25... | collective-permute-start | bytes 3145736 | tf_op jit(solution)/shard_map/ppermute | solution.py:1298
  81.5 17.5 %copy-start.11 = (bf16[16,256]{1,0:T(8,128)(2,1)S(1)}, bf16[16,256]{1,0:T(8,128)(2,1)}, u32[]{:S(2)}) copy-start(bf16[16,256]{1,0:T(8,128)(2,1)} %constant.21.clone.refs_22_) | copy-start | bytes 24580
  155.5 47.5 %collective-permute-start.6 = (bf16[2,1024,512]{2,1,0:T(8,128)(2,1)}, bf16[2,1024,512]{2,1,0:T(8,128)(2,1)}, u32[]{:S(2)}, u32[]{:S(2)}) collective-permute-start(bf16[2,1024,512]{2,1,0:T(8,128)(2,1)} %get-tuple-element.542), channel_id=1, source_target_pairs={{0,16},{1,17},{2,18},{3,19},{4,20},{5,21},{6,22},{7,23},{8,24},{9,... | collective-permute-start | bytes 6291464 | tf_op jit(solution)/shard_map/ppermute | solution.py:1298
  158.1 44.9 %collective-permute-start.5 = (bf16[1024,512]{1,0:T(8,128)(2,1)}, bf16[1024,512]{1,0:T(8,128)(2,1)S(1)}, u32[]{:S(2)}, u32[]{:S(2)}) collective-permute-start(bf16[1024,512]{1,0:T(8,128)(2,1)} %get-tuple-element.530), channel_id=1, source_target_pairs={{16,0},{17,1},{18,2},{19,3},{20,4},{21,5},{22,6},{23,7},{24,8},{25... | collective-permute-start | bytes 3145736 | tf_op jit(solution)/shard_map/ppermute | solution.py:1298
  245.9 41.4 %copy-start = (bf16[1024,512]{1,0:T(8,128)(2,1)S(1)}, bf16[1024,512]{1,0:T(8,128)(2,1)}, u32[]{:S(2)}) copy-start(bf16[1024,512]{1,0:T(8,128)(2,1)} %get-tuple-element.563.shown.shown_t) | copy-start | bytes 3145732
  246.0 41.3 %copy-start.1 = (bf16[400,512]{1,0:T(8,128)(2,1)S(1)}, bf16[400,512]{1,0:T(8,128)(2,1)}, u32[]{:S(2)}) copy-start(bf16[400,512]{1,0:T(8,128)(2,1)} %reduce-scatter.2.cloned.1.call-done.mine) | copy-start | bytes 1228804
  246.0 41.3 %collective-permute-start.7 = (bf16[400,512]{1,0:T(8,128)(2,1)}, bf16[400,512]{1,0:T(8,128)(2,1)S(1)}, u32[]{:S(2)}, u32[]{:S(2)}) collective-permute-start(bf16[400,512]{1,0:T(8,128)(2,1)} %reduce-scatter.2.cloned.1.call-done.mine), channel_id=1, source_target_pairs={{0,16},{16,0},{1,17},{17,1},{2,18},{18,2},{3,19},{19,3},{4,20},{20... | collective-permute-start | bytes 1228808 | tf_op jit(solution)/shard_map/ppermute | solution.py:1298
Sparse Core Ops, SparseCore 0:
  23.3 52.8 all-gather.1
  155.6 88.9 reduce-scatter.1
